TPU v7x, 32 devices: a whole 2x2x4 slice. The times are simulated.
32 devices in a mesh: vis: 2 (over x), grp: 8 (over z, core), enc: 2 (over y).
Axes of the slice: x: 2, y: 2, z: 4, core: 2. Of those that a mesh axis runs over, the one named last changes fastest.
Arguments:
- image_tokens: bfloat16 [8, 256, 6144], P('grp', None, 'enc'), may hold values from -8 to 8
- vision_gain: float32 [6144], P('enc'), may hold values from 0.1 to 1.9
- up_weight: bfloat16 [6144, 12288], P('enc', ('vis', 'grp')), may hold values from -0.078125 to 0.078125
- down_weight: bfloat16 [12288, 6144], P(('vis', 'grp'), 'enc'), may hold values from -0.0546875 to 0.0546875
- project_weight: bfloat16 [6144, 4096], P('enc', 'vis'), may hold values from -0.078125 to 0.078125
- encoder_gain: float32 [4096], P('vis'), may hold values from 0.1 to 1.9
- qkv_weight: bfloat16 [3, 4096, 2048], P(None, 'vis', 'enc'), may hold values from -0.6 to 0.6
- out_weight: bfloat16 [2048, 4096], P('enc', 'vis'), may hold values from -0.5 to 0.5
- captions: bfloat16 [32, 16, 4096], P('grp', 'enc', 'vis'), may hold values from -8 to 8
- cand_counts: int32 [8], replicated, may hold values from 1 to 12, 32 in all
- caption_lengths: int32 [32], P('grp'), may hold values from 1 to 16
Outputs:
- vision_out: bfloat16 [8, 256, 6144], P('grp', None, 'enc')
- caption_out: bfloat16 [32, 16, 4096], P('grp', 'enc', 'vis')
Inputs may be any that keep to these rules, and one draw needn't show every extreme that they name: `cand_counts`: every image has at least one candidate, the counts sum to 32 and the largest is 12.
All inputs are finite; a program needn't handle non-finite values.
Results may differ from a plain program's by a relative error of at most 0.035.
Values may be sent and summed in bfloat16 or wider, within the bound.
No kernel may reach another device: no remote copies, remote signals or barrier semaphores. Data moves between devices by JAX's collectives and lax.ppermute only.
A program may use at most 192 MiB of HBM per device.

v0:
```python
import jax
import jax.numpy as jnp
from jax import lax
from jax.sharding import PartitionSpec as P

DH = 256
CAP = 16
MOSTC = 12


EPSILON = 1e-06
FLOOR = -1e30


def image_of(counts, candidate):
    ends = jnp.cumsum(counts)
    return jnp.sum((candidate[:, None] >= ends[None, :]).astype(jnp.int32), axis=1)


def dot(a, b):
    return jnp.dot(a, b, preferred_element_type=jnp.float32)


def wide(a):
    return a.astype(jnp.float32)


def slim(a):
    return a.astype(jnp.bfloat16)


def shifted(value, axis, step):
    count = lax.axis_size(axis)
    return lax.ppermute(value, axis, [(i, (i + step) % count) for i in range(count)])


def summed(value, axis):
    if lax.axis_size(axis) != 2:
        return lax.psum(value, axis)
    return value + shifted(value, axis, 1)


def joined(value, axis, dim):
    if lax.axis_size(axis) != 2:
        return lax.all_gather(value, axis, axis=dim, tiled=True)
    other = shifted(value, axis, 1)
    first = lax.axis_index(axis) == 0
    return jnp.concatenate(
        [jnp.where(first, value, other), jnp.where(first, other, value)], axis=dim
    )


def on_device(
    image_tokens,
    vision_gain,
    up_weight,
    down_weight,
    project_weight,
    encoder_gain,
    qkv_weight,
    out_weight,
    captions,
    cand_counts,
    caption_lengths,
):
    vis_count = lax.axis_size("vis")
    enc_count = lax.axis_size("enc")
    groups = lax.axis_size("grp")
    vis = lax.axis_index("vis")
    group = lax.axis_index("grp")
    rows, features = image_tokens.shape[1:]
    all_features = features * enc_count
    width = captions.shape[2] * vis_count
    pair = vis_count == 2
    part_rows = rows // vis_count

    cores = 2 if groups % 2 == 0 else 1
    places = groups // cores
    place, core = group // cores, group % cores
    core_swap = [(i, i ^ 1) for i in range(groups)]
    if cores == 2:
        pairs = [[i, i + 1] for i in range(0, groups, 2)]
        up_weight = lax.all_gather(
            up_weight, "grp", axis=1, tiled=True, axis_index_groups=pairs
        )
        down_weight = lax.all_gather(
            down_weight, "grp", axis=0, tiled=True, axis_index_groups=pairs
        )

    def to_place(value, step):
        return lax.ppermute(
            value, "grp", [(i, (i + step * cores) % groups) for i in range(groups)]
        )

    def mine_of(value):
        return lax.dynamic_slice_in_dim(value, vis * part_rows, part_rows, axis=0)

    def by_halves(value):
        if not pair:
            return value
        return jnp.concatenate(
            [mine_of(value), lax.dynamic_slice_in_dim(value, (1 - vis) * part_rows, part_rows, axis=0)]
        )

    def all_rows(mine):
        if not pair:
            return lax.all_gather(mine, "vis", axis=0, tiled=True)
        return jnp.concatenate([mine, shifted(mine, "vis", 1)])

    def my_rows_sum(value):
        if not pair:
            return lax.psum_scatter(value, "vis", scatter_dimension=0, tiled=True)
        return value[:part_rows] + wide(shifted(slim(value[part_rows:]), "vis", 1))

    last = []

    def gated(value):
        return value + last[0].astype(value.dtype) if last else value

    def marked(*values):
        corners = [lax.slice(v, (0,) * v.ndim, (1,) * v.ndim).reshape(()) for v in values]
        last[:] = [sum([wide(corner) for corner in corners]) * 0.0]

    my_tokens = mine_of(image_tokens[0])
    arrived = {1: to_place(my_tokens, 1)} if places > 1 else {}
    words = wide(captions)
    word_power = summed(jnp.sum(words * words, axis=-1), "vis")
    marked(my_tokens)
    tokens = gated(wide(image_tokens[0]))
    row_total, row_squares = summed(
        jnp.stack([jnp.sum(tokens, axis=-1), jnp.sum(tokens * tokens, axis=-1)]), "enc"
    )
    mean = row_total / all_features
    spread = row_squares / all_features - mean * mean
    stats = jnp.stack([mean, lax.rsqrt(spread + EPSILON)], axis=1)
    stats = stats.T
    moved_stats = [to_place(stats, step) if step else stats for step in range(places)]

    def normalized(block, step):
        moved = by_halves(gated(moved_stats[step]).T)
        return slim((wide(block) - moved[:, :1]) * moved[:, 1:] * vision_gain)

    def exchanged(pre):
        if enc_count == 2:
            return pre, shifted(slim(pre), "enc", 1)
        return pre, lax.psum(pre, "enc") - pre

    def up_of(block, step):
        pre = dot(normalized(block, step), up_weight)
        marked(pre)
        return exchanged(pre)

    def down_of(pre, other):
        full = gated(pre) + wide(other)
        out = dot(slim(jax.nn.gelu(full, approximate=False)), down_weight)
        marked(out)
        if pair:
            return out[:part_rows], shifted(slim(out[part_rows:]), "vis", 1)
        kept = lax.psum_scatter(out, "vis", scatter_dimension=0, tiled=True)
        return kept, jnp.zeros_like(kept, jnp.bfloat16)

    inner = qkv_weight.shape[2]
    heads = inner // DH
    shares = vis_count if heads % vis_count == 0 else 1
    share = inner // shares
    split_heads = pair and shares == 2
    word_normed = slim(words * lax.rsqrt(word_power / width + EPSILON)[..., None] * encoder_gain)
    all_words = joined(word_normed, "enc", 1)
    cand_local = all_words.shape[0]
    word_rows = cand_local * CAP
    flat_words = all_words.reshape(word_rows, all_words.shape[2])

    def head_weights(which):
        return lax.dynamic_slice_in_dim(qkv_weight, which * share, share, axis=2)

    def heads_of(block, weight):
        return jnp.einsum("rd,kdh->rkh", block, weight, preferred_element_type=jnp.float32)

    def head_sum(values):
        if shares == 1:
            return lax.psum(values, "vis")
        return lax.psum_scatter(values, "vis", scatter_dimension=2, tiled=True)

    blocks, pres, outs, backs = {}, {}, {}, {}

    def forwarded(step):
        if step < places:
            here = gated(arrived[step]) if step > 1 else arrived[step]
            marked(here)
            if step + 1 < places:
                arrived[step + 1] = to_place(here, 1)
            blocks[step] = all_rows(here)

    def up(step):
        if step < places:
            pres[step] = up_of(blocks[step], step)

    def down(step):
        if step < places:
            outs[step] = down_of(*pres[step])

    def back(step):
        if 0 < step < places:
            total = gated(outs[step][0]) + wide(outs[step][1])
            if step > 1:
                total = total + wide(backs[step - 1])
            total = slim(total)
            marked(total)
            backs[step] = to_place(total, 1)

    blocks[0] = by_halves(image_tokens[0])
    forwarded(1)
    marked(flat_words, *moved_stats[1:], *[arrived[step] for step in (1,) if places > 1])
    up(0)
    forwarded(2)
    up(1)
    forwarded(3)
    flat_words = gated(flat_words)
    if split_heads:
        my_heads, other_heads = head_weights(vis), head_weights(1 - vis)
        sent = slim(heads_of(flat_words, other_heads))
        word_other = shifted(sent, "vis", 1)
        word_kept = heads_of(flat_words, my_heads)
        marked(sent)
    else:
        word_kept = head_sum(heads_of(flat_words, qkv_weight))
    up(2)
    down(1)
    if split_heads:
        word_kept = gated(word_kept) + wide(word_other)
    row_at = jnp.arange(word_rows, dtype=jnp.int32) % CAP
    word_live = row_at < jnp.repeat(caption_lengths, CAP)
    flags = jnp.broadcast_to(word_live[:, None].astype(jnp.bfloat16), (word_rows, 128))
    message = jnp.concatenate([slim(word_kept).reshape(word_rows, 3 * share), flags], axis=1)
    marked(message)
    every_word = lax.all_gather(message, "grp", axis=0, tiled=True)
    if split_heads:
        final_weight = jnp.concatenate(
            [
                lax.dynamic_slice_in_dim(out_weight, vis * share, share, axis=0),
                lax.dynamic_slice_in_dim(out_weight, (1 - vis) * share, share, axis=0),
            ]
        )
        final_weight = gated(final_weight)
        marked(final_weight)
    else:
        final_weight = out_weight
    up(3)
    down(2)
    back(1)
    for step in range(4, places):
        forwarded(step)
        up(step)
        down(step - 1)
    down(places - 1)
    down(0)
    marked(outs[0][0], every_word)
    for step in range(2, places):
        back(step)
    place_rows = cores * word_rows

    cands = groups * cand_local
    most = min(MOSTC, cands)
    ends = jnp.cumsum(cand_counts)
    start = jnp.minimum(ends[group] - cand_counts[group], cands - most)
    near = lax.dynamic_slice_in_dim(every_word, start * CAP, most * CAP, axis=0)
    my_out = wide(my_tokens) + (outs[0][0] + wide(outs[0][1]))
    if places > 1:
        my_out = my_out + wide(backs[places - 1])
    my_vision = slim(my_out)

    def embed(block):
        partial = dot(block, project_weight)
        if enc_count == 2:
            full = partial + wide(shifted(slim(partial), "enc", 1))
        else:
            full = lax.psum(partial, "enc")
        return slim(full * encoder_gain), jnp.sum(full * full, axis=-1)

    if split_heads:
        other_vision = shifted(my_vision, "vis", 1)
        vision_rows = jnp.where(
            vis == 0,
            jnp.concatenate([my_vision, other_vision]),
            jnp.concatenate([other_vision, my_vision]),
        )
        pieces = []
        for block in (my_vision, other_vision):
            scaled, power = embed(block)
            pieces.append(
                (heads_of(scaled, my_heads[1:]), slim(heads_of(scaled, other_heads[1:])), power)
            )
        image_kv = []
        for here, there in ((0, 1), (1, 0)):
            total = pieces[here][0] + wide(shifted(pieces[there][1], "vis", 1))
            power = pieces[here][2] + shifted(pieces[there][2], "vis", 1)
            image_kv.append(
                slim(total * lax.rsqrt(power / width + EPSILON)[:, None, None])
            )
        image_kv = jnp.concatenate(image_kv)
    else:
        vision_rows = joined(my_vision, "vis", 0)
        scaled, power = embed(vision_rows)
        total = head_sum(heads_of(scaled, qkv_weight[1:]))
        power = lax.psum(power, "vis")
        image_kv = slim(total * lax.rsqrt(power / width + EPSILON)[:, None, None])

    live = near[:, 3 * share] > 0
    near = near[:, : 3 * share].reshape(most * CAP, 3, share // DH, DH)
    row_cand = jnp.arange(most * CAP, dtype=jnp.int32) // CAP
    owned = image_of(cand_counts, start + row_cand) == group
    own_allowed = (row_cand[:, None] == row_cand[None, :]) & live[None, :]
    image_kv = image_kv.reshape(rows, 2, share // DH, DH)
    query = near[:, 0]

    def scores_of(keys):
        return jnp.einsum(
            "qhd,khd->hqk", query, keys, preferred_element_type=jnp.float32
        ) * DH ** (-0.5)

    def mixed(weights, values):
        return jnp.einsum(
            "hqk,khd->hqd", slim(weights), values, preferred_element_type=jnp.float32
        )

    image_scores = scores_of(image_kv[:, 0])
    own_scores = jnp.where(own_allowed[None], scores_of(near[:, 1]), FLOOR)
    top = jnp.maximum(
        jnp.max(image_scores, axis=-1, keepdims=True), jnp.max(own_scores, axis=-1, keepdims=True)
    )
    image_weights = jnp.exp(image_scores - top)
    own_weights = jnp.where(own_allowed[None], jnp.exp(own_scores - top), 0.0)
    total = jnp.sum(image_weights, axis=-1, keepdims=True) + jnp.sum(
        own_weights, axis=-1, keepdims=True
    )
    result = (mixed(image_weights, image_kv[:, 1]) + mixed(own_weights, near[:, 2])) / total
    result = jnp.where(owned[:, None, None], slim(result).transpose(1, 0, 2), 0)
    spread_out = lax.dynamic_update_slice_in_dim(
        jnp.zeros((cands * CAP, share), jnp.bfloat16),
        result.reshape(most * CAP, share),
        start * CAP,
        axis=0,
    )
    landed = None
    for step in range(places):
        part = lax.dynamic_slice_in_dim(
            spread_out, (place + step) % places * place_rows, place_rows, axis=0
        )
        part = to_place(part, step) if step else part
        landed = part if landed is None else landed + part
    if cores == 2:
        kept = lax.dynamic_slice_in_dim(landed, core * word_rows, word_rows, axis=0)
        given = lax.dynamic_slice_in_dim(landed, (1 - core) * word_rows, word_rows, axis=0)
        attended = kept + lax.ppermute(given, "grp", core_swap)
    else:
        kept, attended = landed, landed
    if split_heads:
        other = shifted(kept, "vis", 1)
        if cores == 2:
            across = [
                (v * groups + i, (1 - v) * groups + (i ^ 1)) for v in range(2) for i in range(groups)
            ]
            other = other + lax.ppermute(given, ("vis", "grp"), across)
        attended = jnp.concatenate([attended, other], axis=1)
    else:
        if shares > 1:
            attended = lax.all_gather(attended, "vis", axis=1, tiled=True)
    if enc_count == 2:
        enc = lax.axis_index("enc")
        slots = CAP // enc_count
        attended = attended.reshape(cand_local, CAP, inner)

        def branch(which):
            part = lax.dynamic_slice_in_dim(attended, which * slots, slots, axis=1)
            return dot(part.reshape(cand_local * slots, inner), final_weight)

        given = shifted(slim(branch(1 - enc)), "enc", 1)
        words_out = (branch(enc) + wide(given)).reshape(words.shape)
    else:
        partial_words = dot(attended, final_weight).reshape(cand_local, CAP, out_weight.shape[1])
        words_out = lax.psum_scatter(partial_words, "enc", scatter_dimension=1, tiled=True)
    caption_out = slim(words + words_out)
    return (vision_rows[None], caption_out)


def solution(mesh):
    return jax.shard_map(
        on_device,
        mesh=mesh,
        in_specs=(
            P("grp", None, "enc"),
            P("enc"),
            P("enc", ("vis", "grp")),
            P(("vis", "grp"), "enc"),
            P("enc", "vis"),
            P("vis"),
            P(None, "vis", "enc"),
            P("enc", "vis"),
            P("grp", "enc", "vis"),
            P(),
            P("grp"),
        ),
        out_specs=(P("grp", None, "enc"), P("grp", "enc", "vis")),
        check_vma=False,
    )
```

profile of v0, /device:TPU:0, one launch (start us, length us, event | category | flops | bytes accessed | tf_op | source)
XLA Modules:
  0.0 293.2 jit_solution(14924702806225143134)
XLA Ops:
  8.9 2.9 %collective-permute-start.1 = (f32[4,8]{1,0:T(4,128)S(1)}, f32[4,8]{1,0:T(4,128)S(1)}, u32[]{:S(2)}, u32[]{:S(2)}) collective-permute-start(f32[4,8]{1,0:T(4,128)S(1)} %fusion.248), channel_id=1, source_target_pairs={{0,16},{16,0},{1,17},{17,1},{2,18},{18,2},{3,19},{19,3},{4,20},{20... | collective-permute-start | bytes 392 | tf_op jit(solution)/shard_map/ppermute | solution.py:34
  17.9 4.8 %constant_dynamic-slice_fusion.12 = (bf16[512,2048]{1,0:T(8,128)(2,1)S(1)}, bf16[512,2048]{1,0:T(8,128)(2,1)}) fusion(bf16[1024,2048]{1,0:T(8,128)(2,1)} %param.18, s32[]{:T(128)S(6)} %select_n.154, s32[]{:T(128)S(6)} %select_n.155), kind=kLoop, calls=%fused_computation.371 | loop fusion | bytes 8388616 | tf_op jit(solution)/shard_map/dynamic_slice | solution.py:240
  26.2 2.8 collective-permute-start.5
  29.6 4.4 %collective-permute-done.3 = f32[2,256]{1,0:T(2,128)S(1)} collective-permute-done((f32[2,256]{1,0:T(2,128)S(1)}, f32[2,256]{1,0:T(2,128)S(1)}, u32[]{:S(2)}, u32[]{:S(2)}) %collective-permute-start.3) | collective-permute-done | bytes 2080 | tf_op jit(solution)/shard_map/ppermute | solution.py:91
  41.5 9.4 %fusion.437 = (bf16[256,1536]{1,0:T(8,128)(2,1)}, f32[256,1536]{1,0:T(8,128)S(1)}) fusion(bf16[3072,1536]{1,0:T(8,128)(2,1)} %all-gather.4.cloned.1.call-done, bf16[128,3072]{1,0:T(8,128)(2,1)} %get-tuple-element.13, bf16[128,3072]{1,0:T(8,128)(2,1)S(1)} %get-tuple-element.12, f32[3072]{0:T(1024)S(1)} %copy-done.16, f32[256]{0:T(256)S(1)} %bitcast.177, ...), kind=kOutput, calls=%fused_computation.553 | convolution fusion | flops 2422603776 | bytes 13383680 | tf_op jit(solution)/shard_map/dot_general | solution.py:21
  52.2 8.6 %collective-permute-done.7 = bf16[128,3072]{1,0:T(8,128)(2,1)} collective-permute-done((bf16[128,3072]{1,0:T(8,128)(2,1)}, bf16[128,3072]{1,0:T(8,128)(2,1)}, u32[]{:S(2)}, u32[]{:S(2)}) %collective-permute-start.7) | collective-permute-done | bytes 786464 | tf_op jit(solution)/shard_map/ppermute | solution.py:91
  66.3 5.1 %fusion.438 = (bf16[256,1536]{1,0:T(8,128)(2,1)}, f32[256,1536]{1,0:T(8,128)S(1)}) fusion(bf16[3072,1536]{1,0:T(8,128)(2,1)S(1)} %bitcast.186, bf16[128,3072]{1,0:T(8,128)(2,1)} %collective-permute-done.9, bf16[128,3072]{1,0:T(8,128)(2,1)} %collective-permute-done.6, f32[256]{0:T(256)S(1)} %bitcast.179, f32[256]{0:T(256)S(1)} %bitcast.178, ...), kind=kOutput, calls=%fused_computation.554 | convolution fusion | flops 2422603776 | bytes 13383680 | tf_op jit(solution)/shard_map/dot_general | solution.py:21
  73.3 8.2 %collective-permute-done.8 = bf16[128,3072]{1,0:T(8,128)(2,1)S(1)} collective-permute-done((bf16[128,3072]{1,0:T(8,128)(2,1)S(1)}, bf16[128,3072]{1,0:T(8,128)(2,1)S(1)}, u32[]{:S(2)}, u32[]{:S(2)}) %collective-permute-start.8) | collective-permute-done | bytes 786464 | tf_op jit(solution)/shard_map/ppermute | solution.py:91
  89.0 3.6 %fusion.440 = (bf16[256,1536]{1,0:T(8,128)(2,1)}, f32[256,1536]{1,0:T(8,128)S(1)}) fusion(bf16[3072,1536]{1,0:T(8,128)(2,1)S(1)} %bitcast.186, bf16[128,3072]{1,0:T(8,128)(2,1)S(1)} %collective-permute-done.11, bf16[128,3072]{1,0:T(8,128)(2,1)S(1)} %broadcast_add_fusion.1, f32[256]{0:T(256)S(1)} %bitcast.181, f32[256]{0:T(256)S(1)} %bitcast.180, ...), kind=kOutput, calls=%fused_computation.556 | convolution fusion | flops 2422603776 | bytes 13383680 | tf_op jit(solution)/shard_map/dot_general | solution.py:21
  94.9 3.6 %collective-permute-done.12 = bf16[256,1536]{1,0:T(8,128)(2,1)} collective-permute-done((bf16[256,1536]{1,0:T(8,128)(2,1)}, bf16[256,1536]{1,0:T(8,128)(2,1)}, u32[]{:S(2)}, u32[]{:S(2)}) %collective-permute-start.12) | collective-permute-done | bytes 786464 | tf_op jit(solution)/shard_map/ppermute | solution.py:34
  98.5 10.4 %fusion.116 = f32[256,3072]{1,0:T(8,128)S(1)} fusion(bf16[1536,3072]{1,0:T(8,128)(2,1)} %all-gather.6.cloned.1.call-done, bf16[256,1536]{1,0:T(8,128)(2,1)} %collective-permute-done.12, f32[256,1536]{1,0:T(8,128)} %copy-done.24, f32[]{:T(128)} %bitcast.28), kind=kOutput, calls=%fused_computation.171 | convolution fusion | flops 2442657792 | bytes 14942212 | tf_op jit(solution)/shard_map/dot_general | solution.py:21
  121.8 7.0 %fusion.439 = (bf16[256,1536]{1,0:T(8,128)(2,1)S(1)}, f32[256,1536]{1,0:T(8,128)S(1)}) fusion(bf16[3072,1536]{1,0:T(8,128)(2,1)} %all-gather.4.cloned.1.call-done, bf16[128,3072]{1,0:T(8,128)(2,1)} %collective-permute-done.10, bf16[128,3072]{1,0:T(8,128)(2,1)} %broadcast_add_fusion, f32[256]{0:T(256)S(1)} %bitcast.175, f32[256]{0:T(256)S(1)} %bitcast.174, ...), kind=kOutput, calls=%fused_computation.555 | convolution fusion | flops 2422603776 | bytes 13383680 | tf_op jit(solution)/shard_map/dot_general | solution.py:21
  130.6 9.9 %fusion.114 = f32[256,3072]{1,0:T(8,128)S(1)} fusion(bf16[1536,3072]{1,0:T(8,128)(2,1)} %all-gather.6.cloned.1.call-done, bf16[256,1536]{1,0:T(8,128)(2,1)} %collective-permute-done.14, f32[256,1536]{1,0:T(8,128)S(1)} %copy-done.23, f32[]{:T(128)} %bitcast.36), kind=kOutput, calls=%fused_computation.170 | convolution fusion | flops 2442657792 | bytes 14942212 | tf_op jit(solution)/shard_map/dot_general | solution.py:21
  147.7 5.8 %fusion.112 = f32[256,3072]{1,0:T(8,128)S(1)} fusion(bf16[1536,3072]{1,0:T(8,128)(2,1)S(1)} %bitcast.184, bf16[256,1536]{1,0:T(8,128)(2,1)S(1)} %collective-permute-done.16, f32[256,1536]{1,0:T(8,128)S(1)} %get-tuple-element.47, f32[]{:T(128)} %bitcast.38), kind=kOutput, calls=%fused_computation.169 | convolution fusion | flops 2442657792 | bytes 14942212 | tf_op jit(solution)/shard_map/dot_general | solution.py:21
  154.8 7.0 %fusion.110 = f32[256,3072]{1,0:T(8,128)S(1)} fusion(bf16[1536,3072]{1,0:T(8,128)(2,1)S(1)} %bitcast.184, bf16[256,1536]{1,0:T(8,128)(2,1)} %collective-permute-done.17, f32[256,1536]{1,0:T(8,128)S(1)} %copy-done.21, f32[]{:T(128)} %bitcast.39), kind=kOutput, calls=%fused_computation.168 | convolution fusion | flops 2442657792 | bytes 14942212 | tf_op jit(solution)/shard_map/dot_general | solution.py:21
  174.6 10.3 %collective-permute-done.21 = bf16[128,3072]{1,0:T(8,128)(2,1)} collective-permute-done((bf16[128,3072]{1,0:T(8,128)(2,1)}, bf16[128,3072]{1,0:T(8,128)(2,1)}, u32[]{:S(2)}, u32[]{:S(2)}) %collective-permute-start.21) | collective-permute-done | bytes 786464 | tf_op jit(solution)/shard_map/ppermute | solution.py:34
  186.3 2.3 fusion.34
  192.2 4.3 %collective-permute-done.18 = bf16[128,3072]{1,0:T(8,128)(2,1)S(1)} collective-permute-done((bf16[128,3072]{1,0:T(8,128)(2,1)S(1)}, bf16[128,3072]{1,0:T(8,128)(2,1)S(1)}, u32[]{:S(2)}, u32[]{:S(2)}) %collective-permute-start.18) | collective-permute-done | bytes 786464 | tf_op jit(solution)/shard_map/ppermute | solution.py:34
  196.5 8.0 %collective-permute-done.23 = bf16[128,3072]{1,0:T(8,128)(2,1)} collective-permute-done((bf16[128,3072]{1,0:T(8,128)(2,1)}, bf16[128,3072]{1,0:T(8,128)(2,1)}, u32[]{:S(2)}, u32[]{:S(2)}) %collective-permute-start.23) | collective-permute-done | bytes 786464 | tf_op jit(solution)/shard_map/ppermute | solution.py:91
  211.0 7.3 %fusion.441 = (bf16[128,2048]{1,0:T(8,128)(2,1)}, f32[128,2048]{1,0:T(8,128)S(1)}) fusion(bf16[128,3072]{1,0:T(8,128)(2,1)S(1)} %fusion.37, bf16[3072,2048]{1,0:T(8,128)(2,1)} %param.15), kind=kOutput, calls=%fused_computation.557 | convolution fusion | flops 1610874880 | bytes 14942208 | tf_op jit(solution)/shard_map/dot_general | solution.py:21
  220.0 3.0 %fusion.442 = (bf16[128,2048]{1,0:T(8,128)(2,1)}, f32[128,2048]{1,0:T(8,128)}) fusion(bf16[128,3072]{1,0:T(8,128)(2,1)S(1)} %collective-permute-done.24, bf16[3072,2048]{1,0:T(8,128)(2,1)S(1)} %bitcast.155), kind=kOutput, calls=%fused_computation.558 | convolution fusion | flops 1610874880 | bytes 14942208 | tf_op jit(solution)/shard_map/dot_general | solution.py:21
  227.1 4.4 %collective-permute-done.25 = bf16[128,2048]{1,0:T(8,128)(2,1)} collective-permute-done((bf16[128,2048]{1,0:T(8,128)(2,1)}, bf16[128,2048]{1,0:T(8,128)(2,1)}, u32[]{:S(2)}, u32[]{:S(2)}) %collective-permute-start.25) | collective-permute-done | bytes 524320 | tf_op jit(solution)/shard_map/ppermute | solution.py:34
  231.5 5.6 %collective-permute-done.26 = bf16[128,2048]{1,0:T(8,128)(2,1)} collective-permute-done((bf16[128,2048]{1,0:T(8,128)(2,1)}, bf16[128,2048]{1,0:T(8,128)(2,1)}, u32[]{:S(2)}, u32[]{:S(2)}) %collective-permute-start.26) | collective-permute-done | bytes 524320 | tf_op jit(solution)/shard_map/ppermute | solution.py:34
  238.8 3.0 %fusion.95 = bf16[128,2,512]{2,0,1:T(8,128)(2,1)S(1)} fusion(bf16[128,2048,1]{1,0,2:T(8,128)(2,1)S(1)} %get-tuple-element.11, bf16[3,2048,1024]{2,1,0:T(8,128)(2,1)} %param.17, s32[]{:T(128)S(6)} %add.470, s32[]{:T(128)S(6)} %select_n.155), kind=kOutput, calls=%fused_computation.150 | convolution fusion | flops 537001984 | bytes 4980744 | tf_op jit(solution)/shard_map/rd,kdh->rkh/dot_general | solution.py:177
  243.9 3.0 %fusion.92 = bf16[128,2,512]{2,0,1:T(8,128)(2,1)S(1)} fusion(bf16[128,2048,1]{1,0,2:T(8,128)(2,1)S(1)} %get-tuple-element.25, bf16[3,2048,1024]{2,1,0:T(8,128)(2,1)} %param.17, s32[]{:T(128)S(6)} %add.470, s32[]{:T(128)S(6)} %select_n.155), kind=kOutput, calls=%fused_computation.149 | convolution fusion | flops 537001984 | bytes 4980744 | tf_op jit(solution)/shard_map/rd,kdh->rkh/dot_general | solution.py:177
  249.0 4.4 %collective-permute-done.28 = f32[128]{0:T(128)S(1)} collective-permute-done((f32[128]{0:T(128)S(1)}, f32[128]{0:T(128)S(1)}, u32[]{:S(2)}, u32[]{:S(2)}) %collective-permute-start.28) | collective-permute-done | bytes 544 | tf_op jit(solution)/shard_map/ppermute | solution.py:34
  253.4 3.0 %multiply_convert_fusion.10 = bf16[128,2,512]{2,0,1:T(8,128)(2,1)S(1)} fusion(bf16[128,2,512]{2,0,1:T(8,128)(2,1)S(1)} %collective-permute-done.29, f32[128]{0:T(128)S(1)} %add_rsqrt_fusion.2, bf16[128,2048,1]{1,0,2:T(8,128)(2,1)S(1)} %get-tuple-element.25, bf16[3,2048,1024]{2,1,0:T(8,128)(2,1)} %param.17, s32[]{:T(128)S(6)} %add.470, s32[]{:T(128)S(6)} %select_n.154), kind=kOutput, calls=%fused_computation.301 | convolution fusion | flops 537395200 | bytes 5243400 | tf_op jit(solution)/shard_map/rd,kdh->rkh/dot_general | solution.py:177
  256.4 3.0 %multiply_convert_fusion.11 = bf16[128,2,512]{2,0,1:T(8,128)(2,1)S(1)} fusion(bf16[128,2,512]{2,0,1:T(8,128)(2,1)S(1)} %collective-permute-done.27, f32[128]{0:T(128)S(1)} %add_rsqrt_fusion.3, bf16[128,2048,1]{1,0,2:T(8,128)(2,1)S(1)} %get-tuple-element.11, bf16[3,2048,1024]{2,1,0:T(8,128)(2,1)} %param.17, s32[]{:T(128)S(6)} %add.470, s32[]{:T(128)S(6)} %select_n.154), kind=kOutput, calls=%fused_computation.302 | convolution fusion | flops 537395200 | bytes 5243400 | tf_op jit(solution)/shard_map/rd,kdh->rkh/dot_general | solution.py:177
  263.5 4.3 %collective-permute-done.33 = bf16[128,512]{1,0:T(8,128)(2,1)S(1)} collective-permute-done((bf16[128,512]{1,0:T(8,128)(2,1)S(1)}, bf16[128,512]{1,0:T(8,128)(2,1)S(1)}, u32[]{:S(2)}, u32[]{:S(2)}) %collective-permute-start.33) | collective-permute-done | bytes 131104 | tf_op jit(solution)/shard_map/ppermute | solution.py:91
  267.8 2.4 collective-permute-done.31
  276.4 3.2 %convolution_convert_fusion = bf16[32,2048]{1,0:T(8,128)(2,1)S(1)} fusion(bf16[1024,2048]{1,0:T(8,128)(2,1)} %copy-done, bf16[4,16,1024]{2,1,0:T(8,128)(2,1)S(1)} %bitcast.168, s32[]{:T(128)S(6)} %select_n.177), kind=kOutput, calls=%fused_computation.24 | convolution fusion | flops 134283264 | bytes 4390916 | tf_op jit(solution)/shard_map/dot_general | solution.py:21
  282.3 2.4 collective-permute-done.37
  (256 shorter events, 94.7 us)
Async XLA Ops:
  7.2 34.3 %all-gather.4.cloned.1.call-start = ((), (), s32[]{:S(2)}) async-start(), calls=%async_computation | async-start | bytes 14155776 | tf_op jit(solution)/shard_map/all_gather | solution.py:83
  7.9 87.0 %all-gather.6.cloned.1.call-start = ((), (), s32[]{:S(2)}) async-start(), calls=%async_computation.1 | async-start | bytes 14155776 | tf_op jit(solution)/shard_map/all_gather | solution.py:86
  8.7 156.1 %all-gather.8.cloned.1.call-start = ((), (), s32[]{:S(2)}) async-start(), calls=%async_computation.2 | async-start | bytes 1916928 | tf_op jit(solution)/shard_map/all_gather | solution.py:236
  8.9 14.0 %collective-permute-start.1 = (f32[4,8]{1,0:T(4,128)S(1)}, f32[4,8]{1,0:T(4,128)S(1)}, u32[]{:S(2)}, u32[]{:S(2)}) collective-permute-start(f32[4,8]{1,0:T(4,128)S(1)} %fusion.248), channel_id=1, source_target_pairs={{0,16},{16,0},{1,17},{17,1},{2,18},{18,2},{3,19},{19,3},{4,20},{20... | collective-permute-start | bytes 392 | tf_op jit(solution)/shard_map/ppermute | solution.py:34
  12.8 25.9 %collective-permute-start.6 = (bf16[128,3072]{1,0:T(8,128)(2,1)S(1)}, bf16[128,3072]{1,0:T(8,128)(2,1)}, u32[]{:S(2)}, u32[]{:S(2)}) collective-permute-start(bf16[128,3072]{1,0:T(8,128)(2,1)S(1)} %get-tuple-element.12), channel_id=1, source_target_pairs={{0,4},{2,6},{4,8},{6,10},{8,12},{10,14},{12,0},{14,2},{1,5},{3,7},... | collective-permute-start | bytes 2359304 | tf_op jit(solution)/shard_map/ppermute | solution.py:91
  23.0 12.5 %collective-permute-start.2 = (bf16[4,8,2048]{2,1,0:T(8,128)(2,1)S(1)}, bf16[4,8,2048]{2,1,0:T(8,128)(2,1)S(1)}, u32[]{:S(2)}, u32[]{:S(2)}) collective-permute-start(bf16[4,8,2048]{2,1,0:T(8,128)(2,1)S(1)} %fusion.250), channel_id=1, source_target_pairs={{0,1},{1,0},{2,3},{3,2},{4,5},{5,4},{6,7},{7,6},{8,9},{9,8},{10,11... | collective-permute-start | bytes 393224 | tf_op jit(solution)/shard_map/ppermute | solution.py:34
  23.4 10.6 %collective-permute-start.3 = (f32[2,256]{1,0:T(2,128)S(1)}, f32[2,256]{1,0:T(2,128)S(1)}, u32[]{:S(2)}, u32[]{:S(2)}) collective-permute-start(f32[2,256]{1,0:T(2,128)S(1)} %maximum_bitcast_fusion), channel_id=1, source_target_pairs={{0,4},{2,6},{4,8},{6,10},{8,12},{10,14},{12,0},{14,2},{1,5},{3,7},... | collective-permute-start | bytes 6152 | tf_op jit(solution)/shard_map/ppermute | solution.py:91
  25.1 9.5 %collective-permute-start.4 = (f32[2,256]{1,0:T(2,128)S(1)}, f32[2,256]{1,0:T(2,128)S(1)}, u32[]{:S(2)}, u32[]{:S(2)}) collective-permute-start(f32[2,256]{1,0:T(2,128)S(1)} %maximum_bitcast_fusion), channel_id=1, source_target_pairs={{0,8},{2,10},{4,12},{6,14},{8,0},{10,2},{12,4},{14,6},{1,9},{3,11}... | collective-permute-start | bytes 6152 | tf_op jit(solution)/shard_map/ppermute | solution.py:91
  26.2 8.8 %collective-permute-start.5 = (f32[2,256]{1,0:T(2,128)S(1)}, f32[2,256]{1,0:T(2,128)S(1)}, u32[]{:S(2)}, u32[]{:S(2)}) collective-permute-start(f32[2,256]{1,0:T(2,128)S(1)} %maximum_bitcast_fusion), channel_id=1, source_target_pairs={{0,12},{2,14},{4,0},{6,2},{8,4},{10,6},{12,8},{14,10},{1,13},{3,15... | collective-permute-start | bytes 6152 | tf_op jit(solution)/shard_map/ppermute | solution.py:91
  40.5 20.3 %collective-permute-start.7 = (bf16[128,3072]{1,0:T(8,128)(2,1)}, bf16[128,3072]{1,0:T(8,128)(2,1)}, u32[]{:S(2)}, u32[]{:S(2)}) collective-permute-start(bf16[128,3072]{1,0:T(8,128)(2,1)} %collective-permute-done.6), channel_id=1, source_target_pairs={{0,4},{2,6},{4,8},{6,10},{8,12},{10,14},{12,0},{14,2},{1,5},{3,7},... | collective-permute-start | bytes 2359304 | tf_op jit(solution)/shard_map/ppermute | solution.py:91
  40.6 25.6 %collective-permute-start.9 = (bf16[128,3072]{1,0:T(8,128)(2,1)}, bf16[128,3072]{1,0:T(8,128)(2,1)}, u32[]{:S(2)}, u32[]{:S(2)}) collective-permute-start(bf16[128,3072]{1,0:T(8,128)(2,1)} %collective-permute-done.6), channel_id=1, source_target_pairs={{0,16},{16,0},{1,17},{17,1},{2,18},{18,2},{3,19},{19,3},{4,20},{20... | collective-permute-start | bytes 2359304 | tf_op jit(solution)/shard_map/ppermute | solution.py:34
  62.0 19.5 %collective-permute-start.8 = (bf16[128,3072]{1,0:T(8,128)(2,1)S(1)}, bf16[128,3072]{1,0:T(8,128)(2,1)S(1)}, u32[]{:S(2)}, u32[]{:S(2)}) collective-permute-start(bf16[128,3072]{1,0:T(8,128)(2,1)S(1)} %broadcast_add_fusion.1), channel_id=1, source_target_pairs={{0,4},{2,6},{4,8},{6,10},{8,12},{10,14},{12,0},{14,2},{1,5},{3,7},... | collective-permute-start | bytes 2359304 | tf_op jit(solution)/shard_map/ppermute | solution.py:91
  63.1 25.9 %collective-permute-start.11 = (bf16[128,3072]{1,0:T(8,128)(2,1)S(1)}, bf16[128,3072]{1,0:T(8,128)(2,1)S(1)}, u32[]{:S(2)}, u32[]{:S(2)}) collective-permute-start(bf16[128,3072]{1,0:T(8,128)(2,1)S(1)} %broadcast_add_fusion.1), channel_id=1, source_target_pairs={{0,16},{16,0},{1,17},{17,1},{2,18},{18,2},{3,19},{19,3},{4,20},{20... | collective-permute-start | bytes 2359304 | tf_op jit(solution)/shard_map/ppermute | solution.py:34
  64.1 90.7 %collective-permute-start.17 = (bf16[256,1536]{1,0:T(8,128)(2,1)}, bf16[256,1536]{1,0:T(8,128)(2,1)}, u32[]{:S(2)}, u32[]{:S(2)}) collective-permute-start(bf16[256,1536]{1,0:T(8,128)(2,1)} %get-tuple-element.42), channel_id=1, source_target_pairs={{0,1},{1,0},{2,3},{3,2},{4,5},{5,4},{6,7},{7,6},{8,9},{9,8},{10,11... | collective-permute-start | bytes 2359304 | tf_op jit(solution)/shard_map/ppermute | solution.py:34
  72.6 25.9 %collective-permute-start.12 = (bf16[256,1536]{1,0:T(8,128)(2,1)}, bf16[256,1536]{1,0:T(8,128)(2,1)}, u32[]{:S(2)}, u32[]{:S(2)}) collective-permute-start(bf16[256,1536]{1,0:T(8,128)(2,1)} %get-tuple-element.44), channel_id=1, source_target_pairs={{0,1},{1,0},{2,3},{3,2},{4,5},{5,4},{6,7},{7,6},{8,9},{9,8},{10,11... | collective-permute-start | bytes 2359304 | tf_op jit(solution)/shard_map/ppermute | solution.py:34
  82.5 39.3 %collective-permute-start.10 = (bf16[128,3072]{1,0:T(8,128)(2,1)}, bf16[128,3072]{1,0:T(8,128)(2,1)}, u32[]{:S(2)}, u32[]{:S(2)}) collective-permute-start(bf16[128,3072]{1,0:T(8,128)(2,1)} %broadcast_add_fusion), channel_id=1, source_target_pairs={{0,16},{16,0},{1,17},{17,1},{2,18},{18,2},{3,19},{19,3},{4,20},{20... | collective-permute-start | bytes 2359304 | tf_op jit(solution)/shard_map/ppermute | solution.py:34
  87.1 26.7 %collective-permute-start.13 = (bf16[64,3,512]{2,0,1:T(8,128)(2,1)S(1)}, bf16[64,3,512]{2,0,1:T(8,128)(2,1)S(1)}, u32[]{:S(2)}, u32[]{:S(2)}) collective-permute-start(bf16[64,3,512]{2,0,1:T(8,128)(2,1)S(1)} %fusion.105), channel_id=1, source_target_pairs={{0,16},{16,0},{1,17},{17,1},{2,18},{18,2},{3,19},{19,3},{4,20},{20... | collective-permute-start | bytes 589832 | tf_op jit(solution)/shard_map/ppermute | solution.py:34
  111.6 30.2 %collective-permute-start.15 = (bf16[128,3072]{1,0:T(8,128)(2,1)}, bf16[128,3072]{1,0:T(8,128)(2,1)}, u32[]{:S(2)}, u32[]{:S(2)}) collective-permute-start(bf16[128,3072]{1,0:T(8,128)(2,1)} %slice.295), channel_id=1, source_target_pairs={{0,16},{16,0},{1,17},{17,1},{2,18},{18,2},{3,19},{19,3},{4,20},{20... | collective-permute-start | bytes 2359304 | tf_op jit(solution)/shard_map/ppermute | solution.py:34
  112.3 18.3 %collective-permute-start.14 = (bf16[256,1536]{1,0:T(8,128)(2,1)}, bf16[256,1536]{1,0:T(8,128)(2,1)}, u32[]{:S(2)}, u32[]{:S(2)}) collective-permute-start(bf16[256,1536]{1,0:T(8,128)(2,1)} %get-tuple-element.48), channel_id=1, source_target_pairs={{0,1},{1,0},{2,3},{3,2},{4,5},{5,4},{6,7},{7,6},{8,9},{9,8},{10,11... | collective-permute-start | bytes 2359304 | tf_op jit(solution)/shard_map/ppermute | solution.py:34
  128.8 18.8 %collective-permute-start.16 = (bf16[256,1536]{1,0:T(8,128)(2,1)S(1)}, bf16[256,1536]{1,0:T(8,128)(2,1)S(1)}, u32[]{:S(2)}, u32[]{:S(2)}) collective-permute-start(bf16[256,1536]{1,0:T(8,128)(2,1)S(1)} %get-tuple-element.46), channel_id=1, source_target_pairs={{0,1},{1,0},{2,3},{3,2},{4,5},{5,4},{6,7},{7,6},{8,9},{9,8},{10,11... | collective-permute-start | bytes 2359304 | tf_op jit(solution)/shard_map/ppermute | solution.py:34
  145.2 22.1 %collective-permute-start.20 = (bf16[128,3072]{1,0:T(8,128)(2,1)}, bf16[128,3072]{1,0:T(8,128)(2,1)S(1)}, u32[]{:S(2)}, u32[]{:S(2)}) collective-permute-start(bf16[128,3072]{1,0:T(8,128)(2,1)} %fusion.39), channel_id=1, source_target_pairs={{0,4},{2,6},{4,8},{6,10},{8,12},{10,14},{12,0},{14,2},{1,5},{3,7},... | collective-permute-start | bytes 2359304 | tf_op jit(solution)/shard_map/ppermute | solution.py:91
  146.2 21.2 %collective-permute-start.19 = (bf16[128,3072]{1,0:T(8,128)(2,1)S(1)}, bf16[128,3072]{1,0:T(8,128)(2,1)}, u32[]{:S(2)}, u32[]{:S(2)}) collective-permute-start(bf16[128,3072]{1,0:T(8,128)(2,1)S(1)} %slice.293), channel_id=1, source_target_pairs={{0,16},{16,0},{1,17},{17,1},{2,18},{18,2},{3,19},{19,3},{4,20},{20... | collective-permute-start | bytes 2359304 | tf_op jit(solution)/shard_map/ppermute | solution.py:34
  164.2 20.8 %collective-permute-start.21 = (bf16[128,3072]{1,0:T(8,128)(2,1)}, bf16[128,3072]{1,0:T(8,128)(2,1)}, u32[]{:S(2)}, u32[]{:S(2)}) collective-permute-start(bf16[128,3072]{1,0:T(8,128)(2,1)} %slice.292), channel_id=1, source_target_pairs={{0,16},{16,0},{1,17},{17,1},{2,18},{18,2},{3,19},{19,3},{4,20},{20... | collective-permute-start | bytes 2359304 | tf_op jit(solution)/shard_map/ppermute | solution.py:34
  169.4 16.8 %collective-permute-start.22 = (bf16[128,3072]{1,0:T(8,128)(2,1)S(1)}, bf16[128,3072]{1,0:T(8,128)(2,1)S(1)}, u32[]{:S(2)}, u32[]{:S(2)}) collective-permute-start(bf16[128,3072]{1,0:T(8,128)(2,1)S(1)} %fusion.31), channel_id=1, source_target_pairs={{0,4},{2,6},{4,8},{6,10},{8,12},{10,14},{12,0},{14,2},{1,5},{3,7},... | collective-permute-start | bytes 2359304 | tf_op jit(solution)/shard_map/ppermute | solution.py:91
  172.2 24.4 %collective-permute-start.18 = (bf16[128,3072]{1,0:T(8,128)(2,1)S(1)}, bf16[128,3072]{1,0:T(8,128)(2,1)S(1)}, u32[]{:S(2)}, u32[]{:S(2)}) collective-permute-start(bf16[128,3072]{1,0:T(8,128)(2,1)S(1)} %slice.294), channel_id=1, source_target_pairs={{0,16},{16,0},{1,17},{17,1},{2,18},{18,2},{3,19},{19,3},{4,20},{20... | collective-permute-start | bytes 2359304 | tf_op jit(solution)/shard_map/ppermute | solution.py:34
  188.6 15.9 %collective-permute-start.23 = (bf16[128,3072]{1,0:T(8,128)(2,1)}, bf16[128,3072]{1,0:T(8,128)(2,1)}, u32[]{:S(2)}, u32[]{:S(2)}) collective-permute-start(bf16[128,3072]{1,0:T(8,128)(2,1)} %fusion.34), channel_id=1, source_target_pairs={{0,4},{2,6},{4,8},{6,10},{8,12},{10,14},{12,0},{14,2},{1,5},{3,7},... | collective-permute-start | bytes 2359304 | tf_op jit(solution)/shard_map/ppermute | solution.py:91
  206.6 13.4 %collective-permute-start.24 = (bf16[128,3072]{1,0:T(8,128)(2,1)S(1)}, bf16[128,3072]{1,0:T(8,128)(2,1)S(1)}, u32[]{:S(2)}, u32[]{:S(2)}) collective-permute-start(bf16[128,3072]{1,0:T(8,128)(2,1)S(1)} %fusion.37), channel_id=1, source_target_pairs={{0,16},{16,0},{1,17},{17,1},{2,18},{18,2},{3,19},{19,3},{4,20},{20... | collective-permute-start | bytes 2359304 | tf_op jit(solution)/shard_map/ppermute | solution.py:34
  218.3 13.2 %collective-permute-start.25 = (bf16[128,2048]{1,0:T(8,128)(2,1)}, bf16[128,2048]{1,0:T(8,128)(2,1)}, u32[]{:S(2)}, u32[]{:S(2)}) collective-permute-start(bf16[128,2048]{1,0:T(8,128)(2,1)} %get-tuple-element.50), channel_id=1, source_target_pairs={{0,1},{1,0},{2,3},{3,2},{4,5},{5,4},{6,7},{7,6},{8,9},{9,8},{10,11... | collective-permute-start | bytes 1572872 | tf_op jit(solution)/shard_map/ppermute | solution.py:34
  223.0 14.1 %collective-permute-start.26 = (bf16[128,2048]{1,0:T(8,128)(2,1)}, bf16[128,2048]{1,0:T(8,128)(2,1)}, u32[]{:S(2)}, u32[]{:S(2)}) collective-permute-start(bf16[128,2048]{1,0:T(8,128)(2,1)} %get-tuple-element.52), channel_id=1, source_target_pairs={{0,1},{1,0},{2,3},{3,2},{4,5},{5,4},{6,7},{7,6},{8,9},{9,8},{10,11... | collective-permute-start | bytes 1572872 | tf_op jit(solution)/shard_map/ppermute | solution.py:34
  241.8 11.6 %collective-permute-start.29 = (bf16[128,2,512]{2,0,1:T(8,128)(2,1)S(1)}, bf16[128,2,512]{2,0,1:T(8,128)(2,1)S(1)}, u32[]{:S(2)}, u32[]{:S(2)}) collective-permute-start(bf16[128,2,512]{2,0,1:T(8,128)(2,1)S(1)} %fusion.95), channel_id=1, source_target_pairs={{0,16},{16,0},{1,17},{17,1},{2,18},{18,2},{3,19},{19,3},{4,20},{20... | collective-permute-start | bytes 786440 | tf_op jit(solution)/shard_map/ppermute | solution.py:34
  246.9 9.5 %collective-permute-start.27 = (bf16[128,2,512]{2,0,1:T(8,128)(2,1)S(1)}, bf16[128,2,512]{2,0,1:T(8,128)(2,1)S(1)}, u32[]{:S(2)}, u32[]{:S(2)}) collective-permute-start(bf16[128,2,512]{2,0,1:T(8,128)(2,1)S(1)} %fusion.92), channel_id=1, source_target_pairs={{0,16},{16,0},{1,17},{17,1},{2,18},{18,2},{3,19},{19,3},{4,20},{20... | collective-permute-start | bytes 786440 | tf_op jit(solution)/shard_map/ppermute | solution.py:34
  261.6 8.7 %collective-permute-start.31 = (bf16[128,512]{1,0:T(8,128)(2,1)S(1)}, bf16[128,512]{1,0:T(8,128)(2,1)S(1)}, u32[]{:S(2)}, u32[]{:S(2)}) collective-permute-start(bf16[128,512]{1,0:T(8,128)(2,1)S(1)} %get-tuple-element.17), channel_id=1, source_target_pairs={{0,4},{2,6},{4,8},{6,10},{8,12},{10,14},{12,0},{14,2},{1,5},{3,7},... | collective-permute-start | bytes 393224 | tf_op jit(solution)/shard_map/ppermute | solution.py:91
  (49 other events, 494.7 us)
Sparse Core Ops, SparseCore 0:
  9.6 24.5 all-gather.3
  35.7 23.0 all-gather.5
  121.9 26.1 all-gather.7
where the time goes:
time: 298 us; the launch traced here: 293 us
  matrix products  88.6 us (30%)
  waiting for transfers between devices  78.9 us (26%)
  starting transfers between devices  40.3 us (14%)
  local copies, waits for them, and re-layouts  34.4 us (12%)
  between operations  31 us (10%)
  other arithmetic  20 us (7%)
    dot_general x12, matrix products, dot(): return jnp.dot(a, b, preferred_element_type=jnp.float32)  73 us
    ppermute x24, waiting for transfers between devices, shifted(): lax.ppermute(value, axis, [(i, (i + step) % count) for i in range(count)])  37.5 us
    ppermute x12, waiting for transfers between devices, to_place(): lax.ppermute(value, 'grp', [(i, (i + step * cores) % groups) for i in ran...  37.4 us
    ppermute x24, starting transfers between devices, shifted(): lax.ppermute(value, axis, [(i, (i + step) % count) for i in range(count)])  27.7 us
    dot_general x6, matrix products, heads_of(): jnp.einsum('rd,kdh->rkh', block, weight, preferred_element_type=jnp.float32)  14.4 us
    slice x22, local copies, waits for them, and re-layouts, marked(): lax.slice(v, (0,) * v.ndim, (1,) * v.ndim).reshape(())  14.2 us
    ppermute x12, starting transfers between devices, to_place(): lax.ppermute(value, 'grp', [(i, (i + step * cores) % groups) for i in ran...  12 us
    convert_element_type x5, other arithmetic, slim(): return a.astype(jnp.bfloat16)  8.79 us
  transfers between devices with their start and end apart: 41, of which 18 were waited for; matrix products, arithmetic and copies ran while one was open for 42% of the time, Pallas kernels for 0%

commit v1 on v0

--- a/solution.py
+++ b/solution.py
@@ -1,6 +1,10 @@
+import functools
+
 import jax
 import jax.numpy as jnp
 from jax import lax
+from jax.experimental import pallas as pl
+from jax.experimental.pallas import tpu as pltpu
 from jax.sharding import PartitionSpec as P
 
 DH = 256
@@ -10,11 +14,6 @@
 
 EPSILON = 1e-06
 FLOOR = -1e30
-
-
-def image_of(counts, candidate):
-    ends = jnp.cumsum(counts)
-    return jnp.sum((candidate[:, None] >= ends[None, :]).astype(jnp.int32), axis=1)
 
 
 def dot(a, b):
@@ -48,6 +47,128 @@
     return jnp.concatenate(
         [jnp.where(first, value, other), jnp.where(first, other, value)], axis=dim
     )
+
+
+TOKEN = (8, 128)
+HBM = pl.BlockSpec(memory_space=pl.ANY)
+LIGHT = pl.CostEstimate(flops=1024, bytes_accessed=1024, transcendentals=0)
+PARAMS = pltpu.CompilerParams(vmem_limit_bytes=48 * 1024 * 1024)
+
+
+def tile_of(size, most):
+    return most if size % most == 0 else size
+
+
+def up_kernel(cores, steps, mine_ref, theirs_ref, *refs):
+    weights, (out_ref, token_ref, rows_ref) = refs[:cores], refs[-3:]
+    at = pl.program_id(0)
+    half = mine_ref.shape[0]
+
+    @pl.when(at == 0)
+    def _():
+        rows_ref[:half] = mine_ref[...]
+        rows_ref[half:] = theirs_ref[...]
+        token_ref[...] = jnp.zeros(TOKEN, jnp.float32)
+
+    for core in range(cores):
+
+        @pl.when((at >= core * steps) & (at < (core + 1) * steps))
+        def _(core=core):
+            out_ref[...] = slim(dot(rows_ref[...], weights[core][...]))
+
+
+def up_call(halves, weights, after):
+    cores = len(weights)
+    depth, units = weights[0].shape
+    tile = tile_of(units, 256)
+    steps = units // tile
+    rows = 2 * halves[0].shape[0]
+    whole = pl.BlockSpec(halves[0].shape, lambda i: (0, 0))
+
+    def weight_spec(core):
+        return pl.BlockSpec((depth, tile), lambda i: (0, jnp.clip(i - core * steps, 0, steps - 1)))
+
+    return pl.pallas_call(
+        functools.partial(up_kernel, cores, steps),
+        grid=(cores * steps,),
+        in_specs=[whole, whole] + [weight_spec(core) for core in range(cores)] + [HBM] * len(after),
+        out_specs=[
+            pl.BlockSpec((rows, tile), lambda i: (0, i)),
+            pl.BlockSpec(TOKEN, lambda i: (0, 0)),
+        ],
+        out_shape=[
+            jax.ShapeDtypeStruct((rows, cores * units), jnp.bfloat16),
+            jax.ShapeDtypeStruct(TOKEN, jnp.float32),
+        ],
+        scratch_shapes=[pltpu.VMEM((rows, depth), jnp.bfloat16)],
+        compiler_params=PARAMS,
+        cost_estimate=LIGHT,
+    )(*halves, *weights, *after)
+
+
+def down_kernel(cores, steps, own_ref, other_ref, *refs):
+    weights = refs[:cores]
+    kept_ref, sent_ref, token_ref, rest_ref = refs[-4 - cores : -cores]
+    hidden = refs[-cores:]
+    at = pl.program_id(0)
+    tile, columns = weights[0].shape
+    half = kept_ref.shape[0]
+    wide_tile = tile_of(columns, 512)
+
+    def fill(core, step):
+        first = core * steps + step if steps > 1 else core
+        columns_at = pl.ds(pl.multiple_of(first * tile, tile) if steps > 1 else first * tile, tile)
+        total = wide(own_ref[:, columns_at]) + wide(other_ref[:, columns_at])
+        hidden[core][...] = slim(0.5 * total * (1.0 + lax.erf(total * 0.5**0.5)))
+
+    @pl.when(at == 0)
+    def _():
+        fill(0, 0)
+        kept_ref[...] = jnp.zeros_like(kept_ref)
+        rest_ref[...] = jnp.zeros_like(rest_ref)
+        token_ref[...] = jnp.zeros(TOKEN, jnp.float32)
+
+    for core in range(cores):
+        for start in range(0, columns, wide_tile):
+            part = pl.ds(start, wide_tile)
+            term = dot(hidden[core][...], weights[core][:, part])
+            kept_ref[:, part] += term[:half]
+            rest_ref[:, part] += term[half:]
+        if core + 1 < cores:
+            fill(core + 1, at)
+        else:
+            fill(0, jnp.minimum(at + 1, steps - 1))
+
+    @pl.when(at == steps - 1)
+    def _():
+        sent_ref[...] = slim(rest_ref[...])
+
+
+def down_call(own, other, weights, after):
+    cores = len(weights)
+    units, columns = weights[0].shape
+    tile = tile_of(units, 256)
+    steps = units // tile
+    rows = own.shape[0]
+    whole = pl.BlockSpec(own.shape, lambda i: (0, 0))
+    half_spec = pl.BlockSpec((rows // 2, columns), lambda i: (0, 0))
+    return pl.pallas_call(
+        functools.partial(down_kernel, cores, steps),
+        grid=(steps,),
+        in_specs=[whole, whole]
+        + [pl.BlockSpec((tile, columns), lambda i: (i, 0))] * cores
+        + [HBM] * len(after),
+        out_specs=[half_spec, half_spec, pl.BlockSpec(TOKEN, lambda i: (0, 0))],
+        out_shape=[
+            jax.ShapeDtypeStruct((rows // 2, columns), jnp.float32),
+            jax.ShapeDtypeStruct((rows // 2, columns), jnp.bfloat16),
+            jax.ShapeDtypeStruct(TOKEN, jnp.float32),
+        ],
+        scratch_shapes=[pltpu.VMEM((rows // 2, columns), jnp.float32)]
+        + [pltpu.VMEM((rows, tile), jnp.bfloat16) for _ in range(cores)],
+        compiler_params=PARAMS,
+        cost_estimate=LIGHT,
+    )(own, other, *weights, *after)
 
 
 def on_device(
@@ -78,14 +199,13 @@
     places = groups // cores
     place, core = group // cores, group % cores
     core_swap = [(i, i ^ 1) for i in range(groups)]
+    up_weights, down_weights = [up_weight], [down_weight]
     if cores == 2:
-        pairs = [[i, i + 1] for i in range(0, groups, 2)]
-        up_weight = lax.all_gather(
-            up_weight, "grp", axis=1, tiled=True, axis_index_groups=pairs
-        )
-        down_weight = lax.all_gather(
-            down_weight, "grp", axis=0, tiled=True, axis_index_groups=pairs
-        )
+        up_weights.append(lax.ppermute(up_weight, "grp", core_swap))
+        down_weights.append(lax.ppermute(down_weight, "grp", core_swap))
+        if up_weight.shape[1] % 128:
+            up_weights = [jnp.concatenate(up_weights, axis=1)]
+            down_weights = [jnp.concatenate(down_weights)]
 
     def to_place(value, step):
         return lax.ppermute(
@@ -95,69 +215,33 @@
     def mine_of(value):
         return lax.dynamic_slice_in_dim(value, vis * part_rows, part_rows, axis=0)
 
-    def by_halves(value):
-        if not pair:
-            return value
-        return jnp.concatenate(
-            [mine_of(value), lax.dynamic_slice_in_dim(value, (1 - vis) * part_rows, part_rows, axis=0)]
-        )
-
-    def all_rows(mine):
-        if not pair:
-            return lax.all_gather(mine, "vis", axis=0, tiled=True)
-        return jnp.concatenate([mine, shifted(mine, "vis", 1)])
-
-    def my_rows_sum(value):
-        if not pair:
-            return lax.psum_scatter(value, "vis", scatter_dimension=0, tiled=True)
-        return value[:part_rows] + wide(shifted(slim(value[part_rows:]), "vis", 1))
-
-    last = []
+    def halves_of(mine, value):
+        if pair and value is None:
+            return [mine, shifted(mine, "vis", 1)]
+        if pair:
+            return [mine, lax.dynamic_slice_in_dim(value, (1 - vis) * part_rows, part_rows, axis=0)]
+        if value is None:
+            value = lax.all_gather(mine, "vis", axis=0, tiled=True)
+        return [value[: rows // 2], value[rows // 2 :]]
+
+    token = []
 
     def gated(value):
-        return value + last[0].astype(value.dtype) if last else value
-
-    def marked(*values):
-        corners = [lax.slice(v, (0,) * v.ndim, (1,) * v.ndim).reshape(()) for v in values]
-        last[:] = [sum([wide(corner) for corner in corners]) * 0.0]
-
-    my_tokens = mine_of(image_tokens[0])
-    arrived = {1: to_place(my_tokens, 1)} if places > 1 else {}
+        return value + token[0][0, 0].astype(value.dtype) if token else value
+
     words = wide(captions)
     word_power = summed(jnp.sum(words * words, axis=-1), "vis")
-    marked(my_tokens)
-    tokens = gated(wide(image_tokens[0]))
+    tokens = wide(image_tokens[0])
     row_total, row_squares = summed(
         jnp.stack([jnp.sum(tokens, axis=-1), jnp.sum(tokens * tokens, axis=-1)]), "enc"
     )
     mean = row_total / all_features
     spread = row_squares / all_features - mean * mean
-    stats = jnp.stack([mean, lax.rsqrt(spread + EPSILON)], axis=1)
-    stats = stats.T
-    moved_stats = [to_place(stats, step) if step else stats for step in range(places)]
-
-    def normalized(block, step):
-        moved = by_halves(gated(moved_stats[step]).T)
-        return slim((wide(block) - moved[:, :1]) * moved[:, 1:] * vision_gain)
-
-    def exchanged(pre):
-        if enc_count == 2:
-            return pre, shifted(slim(pre), "enc", 1)
-        return pre, lax.psum(pre, "enc") - pre
-
-    def up_of(block, step):
-        pre = dot(normalized(block, step), up_weight)
-        marked(pre)
-        return exchanged(pre)
-
-    def down_of(pre, other):
-        full = gated(pre) + wide(other)
-        out = dot(slim(jax.nn.gelu(full, approximate=False)), down_weight)
-        marked(out)
-        if pair:
-            return out[:part_rows], shifted(slim(out[part_rows:]), "vis", 1)
-        kept = lax.psum_scatter(out, "vis", scatter_dimension=0, tiled=True)
-        return kept, jnp.zeros_like(kept, jnp.bfloat16)
+    normed = slim(
+        (tokens - mean[:, None]) * lax.rsqrt(spread + EPSILON)[:, None] * vision_gain
+    )
+    my_tokens = mine_of(image_tokens[0])
+    my_normed = mine_of(normed)
 
     inner = qkv_weight.shape[2]
     heads = inner // DH
@@ -181,89 +265,116 @@
             return lax.psum(values, "vis")
         return lax.psum_scatter(values, "vis", scatter_dimension=2, tiled=True)
 
-    blocks, pres, outs, backs = {}, {}, {}, {}
+    arrived, blocks, pres, outs, backs = {}, {}, {}, {}, {}
 
     def forwarded(step):
         if step < places:
-            here = gated(arrived[step]) if step > 1 else arrived[step]
-            marked(here)
+            here = arrived[step] if step == 1 else gated(arrived[step])
             if step + 1 < places:
                 arrived[step + 1] = to_place(here, 1)
-            blocks[step] = all_rows(here)
-
-    def up(step):
+            blocks[step] = halves_of(here, None)
+
+    def up(step, *after):
         if step < places:
-            pres[step] = up_of(blocks[step], step)
-
-    def down(step):
+            pre, token[:] = (lambda got: (got[0], [got[1]]))(
+                up_call(blocks[step], up_weights, [*token, *after])
+            )
+            if enc_count == 2:
+                pres[step] = pre, shifted(pre, "enc", 1)
+            else:
+                pres[step] = pre, slim(lax.psum(wide(pre), "enc") - wide(pre))
+
+    def down(step, *after):
         if step < places:
-            outs[step] = down_of(*pres[step])
+            kept, sent, next_token = down_call(*pres[step], down_weights, [*token, *after])
+            token[:] = [next_token]
+            if pair:
+                outs[step] = kept, shifted(sent, "vis", 1)
+            else:
+                out = jnp.concatenate([kept, wide(sent)])
+                kept = lax.psum_scatter(out, "vis", scatter_dimension=0, tiled=True)
+                outs[step] = kept, jnp.zeros_like(kept, jnp.bfloat16)
 
     def back(step):
         if 0 < step < places:
             total = gated(outs[step][0]) + wide(outs[step][1])
             if step > 1:
                 total = total + wide(backs[step - 1])
-            total = slim(total)
-            marked(total)
-            backs[step] = to_place(total, 1)
-
-    blocks[0] = by_halves(image_tokens[0])
+            backs[step] = to_place(slim(total), 1)
+
+    if places > 1:
+        arrived[1] = to_place(my_normed, 1)
     forwarded(1)
-    marked(flat_words, *moved_stats[1:], *[arrived[step] for step in (1,) if places > 1])
+    row_at = jnp.arange(word_rows, dtype=jnp.int32) % CAP
+    word_live = row_at < jnp.repeat(caption_lengths, CAP)
+    flags = jnp.broadcast_to(word_live[:, None].astype(jnp.bfloat16), (word_rows, 128))
+    blocks[0] = halves_of(my_normed, normed)
     up(0)
-    forwarded(2)
-    up(1)
-    forwarded(3)
     flat_words = gated(flat_words)
     if split_heads:
         my_heads, other_heads = head_weights(vis), head_weights(1 - vis)
         sent = slim(heads_of(flat_words, other_heads))
-        word_other = shifted(sent, "vis", 1)
-        word_kept = heads_of(flat_words, my_heads)
-        marked(sent)
+        word_kept = heads_of(flat_words, my_heads) + wide(shifted(sent, "vis", 1))
     else:
         word_kept = head_sum(heads_of(flat_words, qkv_weight))
-    up(2)
-    down(1)
+    forwarded(2)
+    up(1, down_weights[-1], word_kept)
+    message = jnp.concatenate([slim(word_kept).reshape(word_rows, 3 * share), flags], axis=1)
+    messages = [gated(message)]
+    for _ in range(1, places):
+        messages.append(to_place(messages[-1], 1))
+    final_weight = out_weight
     if split_heads:
-        word_kept = gated(word_kept) + wide(word_other)
-    row_at = jnp.arange(word_rows, dtype=jnp.int32) % CAP
-    word_live = row_at < jnp.repeat(caption_lengths, CAP)
-    flags = jnp.broadcast_to(word_live[:, None].astype(jnp.bfloat16), (word_rows, 128))
-    message = jnp.concatenate([slim(word_kept).reshape(word_rows, 3 * share), flags], axis=1)
-    marked(message)
-    every_word = lax.all_gather(message, "grp", axis=0, tiled=True)
-    if split_heads:
-        final_weight = jnp.concatenate(
-            [
-                lax.dynamic_slice_in_dim(out_weight, vis * share, share, axis=0),
-                lax.dynamic_slice_in_dim(out_weight, (1 - vis) * share, share, axis=0),
-            ]
+        final_weight = gated(
+            jnp.concatenate(
+                [
+                    lax.dynamic_slice_in_dim(out_weight, vis * share, share, axis=0),
+                    lax.dynamic_slice_in_dim(out_weight, (1 - vis) * share, share, axis=0),
+                ]
+            )
         )
-        final_weight = gated(final_weight)
-        marked(final_weight)
-    else:
-        final_weight = out_weight
-    up(3)
-    down(2)
+    forwarded(3)
+    up(2, pres[0][1])
+    down(1, messages[min(1, places - 1)])
+    up(3, messages[min(2, places - 1)], final_weight)
+    down(2, messages[min(3, places - 1)])
     back(1)
     for step in range(4, places):
         forwarded(step)
         up(step)
         down(step - 1)
+    word_block = jnp.concatenate(messages)
+    if cores == 2:
+        word_blocks = [word_block, lax.ppermute(word_block, "grp", core_swap)]
+    else:
+        word_blocks = [word_block]
     down(places - 1)
-    down(0)
-    marked(outs[0][0], every_word)
+    down(0, word_blocks[-1])
     for step in range(2, places):
         back(step)
-    place_rows = cores * word_rows
 
     cands = groups * cand_local
     most = min(MOSTC, cands)
     ends = jnp.cumsum(cand_counts)
-    start = jnp.minimum(ends[group] - cand_counts[group], cands - most)
-    near = lax.dynamic_slice_in_dim(every_word, start * CAP, most * CAP, axis=0)
+    start = ends[group] - cand_counts[group]
+    near_ids = start * CAP + jnp.arange(most * CAP, dtype=jnp.int32)
+    owned = near_ids < ends[group] * CAP
+
+    def ids_of(core_at, sign):
+        steps = jnp.arange(places, dtype=jnp.int32)[:, None]
+        first = ((place + sign * steps) % places * cores + core_at) * word_rows
+        return (first + jnp.arange(word_rows, dtype=jnp.int32)[None]).reshape(-1)
+
+    core_order = [core, 1 - core][:cores]
+    near = 0.0
+    for core_at, block in zip(core_order, word_blocks):
+        pick = near_ids[:, None] == ids_of(core_at, -1)[None, :]
+        near = near + dot(pick.astype(jnp.bfloat16), block)
+    near = slim(near)
+    place_ids = jnp.concatenate(
+        [ids_of(core_at, 1).reshape(places, word_rows) for core_at in core_order], axis=1
+    ).reshape(-1)
+    put = slim((place_ids[:, None] == near_ids[None, :]) & owned[None, :])
     my_out = wide(my_tokens) + (outs[0][0] + wide(outs[0][1]))
     if places > 1:
         my_out = my_out + wide(backs[places - 1])
@@ -308,7 +419,6 @@
     live = near[:, 3 * share] > 0
     near = near[:, : 3 * share].reshape(most * CAP, 3, share // DH, DH)
     row_cand = jnp.arange(most * CAP, dtype=jnp.int32) // CAP
-    owned = image_of(cand_counts, start + row_cand) == group
     own_allowed = (row_cand[:, None] == row_cand[None, :]) & live[None, :]
     image_kv = image_kv.reshape(rows, 2, share // DH, DH)
     query = near[:, 0]
@@ -334,26 +444,16 @@
         own_weights, axis=-1, keepdims=True
     )
     result = (mixed(image_weights, image_kv[:, 1]) + mixed(own_weights, near[:, 2])) / total
-    result = jnp.where(owned[:, None, None], slim(result).transpose(1, 0, 2), 0)
-    spread_out = lax.dynamic_update_slice_in_dim(
-        jnp.zeros((cands * CAP, share), jnp.bfloat16),
-        result.reshape(most * CAP, share),
-        start * CAP,
-        axis=0,
-    )
-    landed = None
-    for step in range(places):
-        part = lax.dynamic_slice_in_dim(
-            spread_out, (place + step) % places * place_rows, place_rows, axis=0
-        )
-        part = to_place(part, step) if step else part
-        landed = part if landed is None else landed + part
+    result = slim(result).transpose(1, 0, 2).reshape(most * CAP, share)
+    spread_out = slim(dot(put, result)).reshape(places, cores * word_rows, share)
+    landed = spread_out[0]
+    for step in range(1, places):
+        landed = landed + to_place(spread_out[step], step)
+    kept = landed[:word_rows]
+    attended = kept
     if cores == 2:
-        kept = lax.dynamic_slice_in_dim(landed, core * word_rows, word_rows, axis=0)
-        given = lax.dynamic_slice_in_dim(landed, (1 - core) * word_rows, word_rows, axis=0)
+        given = landed[word_rows:]
         attended = kept + lax.ppermute(given, "grp", core_swap)
-    else:
-        kept, attended = landed, landed
     if split_heads:
         other = shifted(kept, "vis", 1)
         if cores == 2:

time: 298 us -> 300 us (level); the launches traced: 293 us -> 299 us
  Pallas kernels: 0 us -> 56.4 us
  matrix products: 88.6 us -> 37.2 us
  waiting for transfers between devices: 78.9 us -> 124 us
  between operations: 31 us -> 3.33 us
  local copies, waits for them, and re-layouts: 34.4 us -> 14.4 us
  other arithmetic: 20 us -> 25.8 us
    dot_general x12 -> x7, matrix products: 73 us -> 16 us  [dot(): return jnp.dot(a, b, preferred_element_type=jnp.float32)]
    pallas_call x0 -> x8, Pallas kernels: none -> 56.4 us  [the longest x4 29.7 us: up_call(): pl.pallas_call(functools.partial(up_kernel, cores, steps), grid=(cores *...]
    ppermute x12, waiting for transfers between devices: 37.4 us -> 68.4 us  [to_place(): lax.ppermute(value, 'grp', [(i, (i + step * cores) % groups) for i in ran...]
    ppermute x24, waiting for transfers between devices: 37.5 us -> 54.3 us  [shifted(): lax.ppermute(value, axis, [(i, (i + step) % count) for i in range(count)])]
    slice x26 -> x6, local copies, waits for them, and re-layouts: 18.4 us -> 2.14 us  [the longest x4 2.1 us: gated(): return value + token[0][0, 0].astype(value.dtype) if token else value]
    dot_general x6, matrix products: 14.4 us -> 20 us  [heads_of(): jnp.einsum('rd,kdh->rkh', block, weight, preferred_element_type=jnp.float32)]
    ppermute x12, starting transfers between devices: 12 us -> 8.63 us  [to_place(): lax.ppermute(value, 'grp', [(i, (i + step * cores) % groups) for i in ran...]
    convert_element_type x5 -> x7, other arithmetic: 8.79 us -> 11.9 us  [slim(): return a.astype(jnp.bfloat16)]
  transfers between devices with their start and end apart: 41 -> 41, of which waited for: 18 -> 18; matrix products, arithmetic and copies ran while one was open for 42% -> 20% of each run, Pallas kernels for 0% -> 19%
where the time goes in v1:
time: 300 us; the launch traced here: 299 us
  waiting for transfers between devices  124 us (41%)
  Pallas kernels  56.4 us (19%)
  starting transfers between devices  38.1 us (13%)
  matrix products  37.2 us (12%)
  other arithmetic  25.8 us (9%)
  local copies, waits for them, and re-layouts  14.4 us (5%)
  between operations  3.33 us (1%)
    ppermute x12, waiting for transfers between devices, to_place(): lax.ppermute(value, 'grp', [(i, (i + step * cores) % groups) for i in ran...  68.4 us
    ppermute x24, waiting for transfers between devices, shifted(): lax.ppermute(value, axis, [(i, (i + step) % count) for i in range(count)])  54.3 us
    pallas_call x4, Pallas kernels, up_call(): pl.pallas_call(functools.partial(up_kernel, cores, steps), grid=(cores *...  29.7 us
    ppermute x24, starting transfers between devices, shifted(): lax.ppermute(value, axis, [(i, (i + step) % count) for i in range(count)])  27.2 us
    pallas_call x4, Pallas kernels, down_call(): pl.pallas_call(functools.partial(down_kernel, cores, steps), grid=(steps,...  26.7 us
    dot_general x6, matrix products, heads_of(): jnp.einsum('rd,kdh->rkh', block, weight, preferred_element_type=jnp.float32)  20 us
    dot_general x7, matrix products, dot(): return jnp.dot(a, b, preferred_element_type=jnp.float32)  16 us
    convert_element_type x7, other arithmetic, slim(): return a.astype(jnp.bfloat16)  11.9 us
  transfers between devices with their start and end apart: 41, of which 18 were waited for; matrix products, arithmetic and copies ran while one was open for 20% of the time, Pallas kernels for 19%

profile of v1, /device:TPU:0, one launch (start us, length us, event | category | flops | bytes accessed | tf_op | source)
XLA Modules:
  0.0 299.1 jit_solution(2668214672124176354)
XLA Ops:
  12.3 18.2 %collective-permute-done.4.mine_ref = bf16[128,3072]{1,0:T(8,128)(2,1)S(1)} collective-permute-done((bf16[128,3072]{1,0:T(8,128)(2,1)S(1)}, bf16[128,3072]{1,0:T(8,128)(2,1)S(1)}, u32[]{:S(2)}, u32[]{:S(2)}) %collective-permute-start.4) | collective-permute-done | bytes 786464 | tf_op jit(solution)/shard_map/ppermute | solution.py:211
  31.3 7.4 %shard_map.122 = (bf16[256,1536]{1,0:T(8,128)(2,1)S(1)}, f32[8,128]{1,0:T(8,128)S(1)}) custom-call(bf16[128,3072]{1,0:T(8,128)(2,1)S(1)} %get-tuple-element.51.mine_ref, bf16[128,3072]{1,0:T(8,128)(2,1)S(1)} %get-tuple-element.50.theirs_ref, bf16[3072,768]{1,0:T(8,128)(2,1)} %refs_0_.12, bf16[3072,768]{1,0:T(8,128)(2,1)} %collective-permute-done.1.refs_1_), custom_call_target="tpu_custom_call" | custom-call | flops 1024 | bytes 1024 | tf_op jit(solution)/shard_map/pallas_call | solution.py:91
  40.0 4.1 %fusion.31 = bf16[64,3,512]{2,0,1:T(8,128)(2,1)S(1)} fusion(bf16[64,2048,1]{1,0,2:T(8,128)(2,1)S(1)} %bitcast.109, bf16[3,2048,1024]{2,1,0:T(8,128)(2,1)} %param.17, s32[]{:T(128)S(6)} %select_n.131), kind=kOutput, calls=%fused_computation.41 | convolution fusion | flops 402751488 | bytes 6750212 | tf_op jit(solution)/shard_map/rd,kdh->rkh/dot_general | solution.py:261
  45.8 5.7 %collective-permute-done.5 = bf16[128,3072]{1,0:T(8,128)(2,1)S(1)} collective-permute-done((bf16[128,3072]{1,0:T(8,128)(2,1)S(1)}, bf16[128,3072]{1,0:T(8,128)(2,1)S(1)}, u32[]{:S(2)}, u32[]{:S(2)}) %collective-permute-start.5) | collective-permute-done | bytes 786464 | tf_op jit(solution)/shard_map/ppermute | solution.py:211
  52.4 4.5 %collective-permute-done.10 = bf16[64,3,512]{2,1,0:T(4,128)(2,1)S(1)} collective-permute-done((bf16[64,3,512]{2,1,0:T(4,128)(2,1)S(1)}, bf16[64,3,512]{2,1,0:T(4,128)(2,1)S(1)}, u32[]{:S(2)}, u32[]{:S(2)}) %collective-permute-start.10) | collective-permute-done | bytes 196640 | tf_op jit(solution)/shard_map/ppermute | solution.py:33
  57.2 4.0 %fusion.2 = f32[64,3,512]{2,0,1:T(8,128)S(1)} fusion(bf16[64,2048,1]{1,0,2:T(8,128)(2,1)S(1)} %bitcast.110, bf16[3,2048,1024]{2,1,0:T(8,128)(2,1)} %param.17, s32[]{:T(128)S(6)} %select_n.130), kind=kOutput, calls=%fused_computation.2 | convolution fusion | flops 402653184 | bytes 6946820 | tf_op jit(solution)/shard_map/rd,kdh->rkh/dot_general | solution.py:261
  61.7 7.4 %shard_map.123 = (bf16[256,1536]{1,0:T(8,128)(2,1)S(1)}, f32[8,128]{1,0:T(8,128)S(1)}) custom-call(bf16[128,3072]{1,0:T(8,128)(2,1)S(1)} %collective-permute-done.4.mine_ref, bf16[128,3072]{1,0:T(8,128)(2,1)S(1)} %collective-permute-done.7.theirs_ref, bf16[3072,768]{1,0:T(8,128)(2,1)} %refs_0_.12, bf16[3072,768]{1,0:T(8,128)(2,1)} %collective-permute-done.1.refs_1_, ...), custom_call_target="tpu_custom_call" | custom-call | flops 1024 | bytes 1024 | tf_op jit(solution)/shard_map/pallas_call | solution.py:91
  73.5 4.7 %collective-permute-done.14.refs_3_ = bf16[64,1664]{1,0:T(8,128)(2,1)S(1)} collective-permute-done((bf16[64,1664]{1,0:T(8,128)(2,1)S(1)}, bf16[64,1664]{1,0:T(8,128)(2,1)S(1)}, u32[]{:S(2)}, u32[]{:S(2)}) %collective-permute-start.14) | collective-permute-done | bytes 213024 | tf_op jit(solution)/shard_map/ppermute | solution.py:211
  78.2 7.4 %shard_map.124 = (bf16[256,1536]{1,0:T(8,128)(2,1)S(1)}, f32[8,128]{1,0:T(8,128)S(1)}) custom-call(bf16[128,3072]{1,0:T(8,128)(2,1)S(1)} %broadcast_add_fusion.1.mine_ref, bf16[128,3072]{1,0:T(8,128)(2,1)S(1)} %collective-permute-done.13.theirs_ref, bf16[3072,768]{1,0:T(8,128)(2,1)} %refs_0_.12, bf16[3072,768]{1,0:T(8,128)(2,1)} %collective-permute-done.1.refs_1_, ...), custom_call_target="tpu_custom_call" | custom-call | flops 1024 | bytes 1024 | tf_op jit(solution)/shard_map/pallas_call | solution.py:91
  89.4 4.7 %collective-permute-done.12.other_ref = bf16[256,1536]{1,0:T(8,128)(2,1)S(1)} collective-permute-done((bf16[256,1536]{1,0:T(8,128)(2,1)S(1)}, bf16[256,1536]{1,0:T(8,128)(2,1)S(1)}, u32[]{:S(2)}, u32[]{:S(2)}) %collective-permute-start.12) | collective-permute-done | bytes 786464 | tf_op jit(solution)/shard_map/ppermute | solution.py:33
  94.1 6.2 %shard_map.125 = (f32[128,3072]{1,0:T(8,128)S(1)}, bf16[128,3072]{1,0:T(8,128)(2,1)S(1)}, f32[8,128]{1,0:T(8,128)S(1)}) custom-call(bf16[256,1536]{1,0:T(8,128)(2,1)S(1)} %get-tuple-element.25.own_ref, bf16[256,1536]{1,0:T(8,128)(2,1)S(1)} %collective-permute-done.12.other_ref, bf16[768,3072]{1,0:T(8,128)(2,1)} %refs_0_.15, ...), custom_call_target="tpu_custom_call" | custom-call | flops 1024 | bytes 1024 | tf_op jit(solution)/shard_map/pallas_call | solution.py:155
  104.6 3.2 %maximum_add_fusion.refs_4_ = bf16[1024,2048]{1,0:T(8,128)(2,1)} fusion(bf16[512,2048]{1,0:T(8,128)(2,1)S(1)} %get-tuple-element.45, bf16[512,2048]{1,0:T(8,128)(2,1)S(1)} %get-tuple-element.44, bf16[]{:T(256)} %bitcast.10), kind=kLoop, calls=%fused_computation.4 | loop fusion | flops 12582912 | bytes 8388610 | tf_op jit(solution)/shard_map/add | solution.py:230
  111.8 7.4 %shard_map.126 = (bf16[256,1536]{1,0:T(8,128)(2,1)S(1)}, f32[8,128]{1,0:T(8,128)S(1)}) custom-call(bf16[128,3072]{1,0:T(8,128)(2,1)S(1)} %broadcast_add_fusion.mine_ref, bf16[128,3072]{1,0:T(8,128)(2,1)S(1)} %collective-permute-done.11.theirs_ref, bf16[3072,768]{1,0:T(8,128)(2,1)} %refs_0_.12, bf16[3072,768]{1,0:T(8,128)(2,1)} %collective-permute-done.1.refs_1_, ...), custom_call_target="tpu_custom_call" | custom-call | flops 1024 | bytes 1024 | tf_op jit(solution)/shard_map/pallas_call | solution.py:91
  119.2 7.1 %shard_map.127 = (f32[128,3072]{1,0:T(8,128)S(1)}, bf16[128,3072]{1,0:T(8,128)(2,1)}, f32[8,128]{1,0:T(8,128)S(1)}) custom-call(bf16[256,1536]{1,0:T(8,128)(2,1)S(1)} %get-tuple-element.29.own_ref, bf16[256,1536]{1,0:T(8,128)(2,1)S(1)} %collective-permute-done.17.other_ref, bf16[768,3072]{1,0:T(8,128)(2,1)} %refs_0_.15, ...), custom_call_target="tpu_custom_call" | custom-call | flops 1024 | bytes 1024 | tf_op jit(solution)/shard_map/pallas_call | solution.py:155
  131.9 17.8 %collective-permute-done.16.other_ref = bf16[256,1536]{1,0:T(8,128)(2,1)S(1)} collective-permute-done((bf16[256,1536]{1,0:T(8,128)(2,1)S(1)}, bf16[256,1536]{1,0:T(8,128)(2,1)S(1)}, u32[]{:S(2)}, u32[]{:S(2)}) %collective-permute-start.16) | collective-permute-done | bytes 786464 | tf_op jit(solution)/shard_map/ppermute | solution.py:33
  149.7 7.1 %shard_map.128 = (f32[128,3072]{1,0:T(8,128)S(1)}, bf16[128,3072]{1,0:T(8,128)(2,1)}, f32[8,128]{1,0:T(8,128)S(1)}) custom-call(bf16[256,1536]{1,0:T(8,128)(2,1)S(1)} %get-tuple-element.28.own_ref, bf16[256,1536]{1,0:T(8,128)(2,1)S(1)} %collective-permute-done.16.other_ref, bf16[768,3072]{1,0:T(8,128)(2,1)} %refs_0_.15, ...), custom_call_target="tpu_custom_call" | custom-call | flops 1024 | bytes 1024 | tf_op jit(solution)/shard_map/pallas_call | solution.py:155
  158.3 6.3 %shard_map.129 = (f32[128,3072]{1,0:T(8,128)S(1)}, bf16[128,3072]{1,0:T(8,128)(2,1)S(1)}, f32[8,128]{1,0:T(8,128)S(1)}) custom-call(bf16[256,1536]{1,0:T(8,128)(2,1)S(1)} %copy-done.8, bf16[256,1536]{1,0:T(8,128)(2,1)S(1)} %collective-permute-done.2.refs_3_.other_ref, bf16[768,3072]{1,0:T(8,128)(2,1)} %refs_0_.15, ...), custom_call_target="tpu_custom_call" | custom-call | flops 1024 | bytes 1024 | tf_op jit(solution)/shard_map/pallas_call | solution.py:155
  165.1 3.2 %add_convert_fusion.1 = bf16[128,3072]{1,0:T(8,128)(2,1)} fusion(bf16[128,3072]{1,0:T(8,128)(2,1)} %collective-permute-done.24, bf16[128,3072]{1,0:T(8,128)(2,1)} %collective-permute-done.22, f32[128,3072]{1,0:T(8,128)S(1)} %copy-done.1, f32[]{:T(128)} %bitcast.11), kind=kLoop, calls=%fused_computation.29 | loop fusion | flops 2359296 | bytes 3932164 | tf_op jit(solution)/shard_map/convert_element_type | solution.py:28
  173.7 5.0 %collective-permute-done.21 = bf16[128,3072]{1,0:T(8,128)(2,1)} collective-permute-done((bf16[128,3072]{1,0:T(8,128)(2,1)}, bf16[128,3072]{1,0:T(8,128)(2,1)}, u32[]{:S(2)}, u32[]{:S(2)}) %collective-permute-start.21) | collective-permute-done | bytes 786464 | tf_op jit(solution)/shard_map/ppermute | solution.py:33
  178.8 10.5 %collective-permute-done.25 = bf16[128,3072]{1,0:T(8,128)(2,1)S(1)} collective-permute-done((bf16[128,3072]{1,0:T(8,128)(2,1)}, bf16[128,3072]{1,0:T(8,128)(2,1)S(1)}, u32[]{:S(2)}, u32[]{:S(2)}) %collective-permute-start.25) | collective-permute-done | bytes 786464 | tf_op jit(solution)/shard_map/ppermute | solution.py:211
  190.2 3.8 %add_convert_fusion = bf16[128,3072]{1,0:T(8,128)(2,1)} fusion(bf16[128,3072]{1,0:T(8,128)(2,1)} %copy-done.18, bf16[128,3072]{1,0:T(8,128)(2,1)} %collective-permute-done.21, f32[128,3072]{1,0:T(8,128)} %copy-done.2, f32[]{:T(128)} %bitcast.11), kind=kLoop, calls=%fused_computation.28 | loop fusion | flops 2359296 | bytes 3932164 | tf_op jit(solution)/shard_map/convert_element_type | solution.py:28
  195.0 19.1 %collective-permute-done.26 = bf16[128,3072]{1,0:T(8,128)(2,1)} collective-permute-done((bf16[128,3072]{1,0:T(8,128)(2,1)}, bf16[128,3072]{1,0:T(8,128)(2,1)}, u32[]{:S(2)}, u32[]{:S(2)}) %collective-permute-start.26) | collective-permute-done | bytes 786464 | tf_op jit(solution)/shard_map/ppermute | solution.py:211
  217.4 7.3 %fusion.95 = (bf16[128,2048]{1,0:T(8,128)(2,1)}, f32[128,2048]{1,0:T(8,128)S(1)}) fusion(bf16[128,3072]{1,0:T(8,128)(2,1)S(1)} %fusion.20, bf16[3072,2048]{1,0:T(8,128)(2,1)} %param.15), kind=kOutput, calls=%fused_computation.163 | convolution fusion | flops 1610874880 | bytes 14942208 | tf_op jit(solution)/shard_map/dot_general | solution.py:20
  225.7 7.6 %collective-permute-done.27 = bf16[128,3072]{1,0:T(8,128)(2,1)S(1)} collective-permute-done((bf16[128,3072]{1,0:T(8,128)(2,1)S(1)}, bf16[128,3072]{1,0:T(8,128)(2,1)S(1)}, u32[]{:S(2)}, u32[]{:S(2)}) %collective-permute-start.27) | collective-permute-done | bytes 786464 | tf_op jit(solution)/shard_map/ppermute | solution.py:33
  240.9 6.4 %collective-permute-done.29 = bf16[128,2048]{1,0:T(8,128)(2,1)} collective-permute-done((bf16[128,2048]{1,0:T(8,128)(2,1)}, bf16[128,2048]{1,0:T(8,128)(2,1)}, u32[]{:S(2)}, u32[]{:S(2)}) %collective-permute-start.29) | collective-permute-done | bytes 524320 | tf_op jit(solution)/shard_map/ppermute | solution.py:33
  251.1 3.1 %fusion.24 = bf16[128,2,512]{2,0,1:T(8,128)(2,1)S(1)} fusion(bf16[128,2048,1]{1,0,2:T(8,128)(2,1)S(1)} %get-tuple-element.49, bf16[3,2048,1024]{2,1,0:T(8,128)(2,1)} %param.17, s32[]{:T(128)S(6)} %add.487, s32[]{:T(128)S(6)} %select_n.131), kind=kOutput, calls=%fused_computation.33 | convolution fusion | flops 537001984 | bytes 4980744 | tf_op jit(solution)/shard_map/rd,kdh->rkh/dot_general | solution.py:261
  254.2 3.1 %fusion.21 = bf16[128,2,512]{2,0,1:T(8,128)(2,1)S(1)} fusion(bf16[128,2048,1]{1,0,2:T(8,128)(2,1)S(1)} %get-tuple-element.65, bf16[3,2048,1024]{2,1,0:T(8,128)(2,1)} %param.17, s32[]{:T(128)S(6)} %add.487, s32[]{:T(128)S(6)} %select_n.131), kind=kOutput, calls=%fused_computation.32 | convolution fusion | flops 537001984 | bytes 4980744 | tf_op jit(solution)/shard_map/rd,kdh->rkh/dot_general | solution.py:261
  259.4 4.4 %collective-permute-done.30 = bf16[128,2,512]{2,0,1:T(8,128)(2,1)S(1)} collective-permute-done((bf16[128,2,512]{2,0,1:T(8,128)(2,1)S(1)}, bf16[128,2,512]{2,0,1:T(8,128)(2,1)S(1)}, u32[]{:S(2)}, u32[]{:S(2)}) %collective-permute-start.30) | collective-permute-done | bytes 262176 | tf_op jit(solution)/shard_map/ppermute | solution.py:33
  271.9 3.8 %collective-permute-start.36 = (bf16[128,512]{1,0:T(8,128)(2,1)S(1)}, bf16[128,512]{1,0:T(8,128)(2,1)S(1)}, u32[]{:S(2)}, u32[]{:S(2)}) collective-permute-start(bf16[128,512]{1,0:T(8,128)(2,1)S(1)} %get-tuple-element.56), channel_id=1, source_target_pairs={{0,12},{2,14},{4,0},{6,2},{8,4},{10,6},{12,8},{14,10},{1,13},{3,15... | collective-permute-start | bytes 393224 | tf_op jit(solution)/shard_map/ppermute | solution.py:211
  275.8 3.0 %collective-permute-done.34 = bf16[128,512]{1,0:T(8,128)(2,1)S(1)} collective-permute-done((bf16[128,512]{1,0:T(8,128)(2,1)S(1)}, bf16[128,512]{1,0:T(8,128)(2,1)S(1)}, u32[]{:S(2)}, u32[]{:S(2)}) %collective-permute-start.34) | collective-permute-done | bytes 131104 | tf_op jit(solution)/shard_map/ppermute | solution.py:211
  278.8 4.1 %collective-permute-done.35 = bf16[128,512]{1,0:T(8,128)(2,1)S(1)} collective-permute-done((bf16[128,512]{1,0:T(8,128)(2,1)S(1)}, bf16[128,512]{1,0:T(8,128)(2,1)S(1)}, u32[]{:S(2)}, u32[]{:S(2)}) %collective-permute-start.35) | collective-permute-done | bytes 131104 | tf_op jit(solution)/shard_map/ppermute | solution.py:211
  289.1 3.2 %convolution_convert_fusion = bf16[32,2048]{1,0:T(8,128)(2,1)S(1)} fusion(bf16[1024,2048]{1,0:T(8,128)(2,1)} %maximum_add_fusion.refs_4_, bf16[4,16,1024]{2,1,0:T(8,128)(2,1)S(1)} %bitcast.113, s32[]{:T(128)S(6)} %select_n.143), kind=kOutput, calls=%fused_computation.23 | convolution fusion | flops 134283264 | bytes 4390916 | tf_op jit(solution)/shard_map/dot_general | solution.py:20
  (204 shorter events, 84.8 us)
Async XLA Ops:
  0.7 30.6 %collective-permute-start.1 = (bf16[3072,768]{1,0:T(8,128)(2,1)}, bf16[3072,768]{1,0:T(8,128)(2,1)}, u32[]{:S(2)}, u32[]{:S(2)}) collective-permute-start(bf16[3072,768]{1,0:T(8,128)(2,1)} %refs_0_.12), channel_id=1, source_target_pairs={{0,2},{2,0},{4,6},{6,4},{8,10},{10,8},{12,14},{14,12},{1,3},{3,1},... | collective-permute-start | bytes 14155784 | tf_op jit(solution)/shard_map/ppermute | solution.py:204
  7.6 54.0 %collective-permute-start.3 = (bf16[768,3072]{1,0:T(8,128)(2,1)}, bf16[768,3072]{1,0:T(8,128)(2,1)}, u32[]{:S(2)}, u32[]{:S(2)}) collective-permute-start(bf16[768,3072]{1,0:T(8,128)(2,1)} %refs_0_.15), channel_id=1, source_target_pairs={{0,2},{2,0},{4,6},{6,4},{8,10},{10,8},{12,14},{14,12},{1,3},{3,1},... | collective-permute-start | bytes 14155784 | tf_op jit(solution)/shard_map/ppermute | solution.py:205
  8.7 21.9 %collective-permute-start.4 = (bf16[128,3072]{1,0:T(8,128)(2,1)S(1)}, bf16[128,3072]{1,0:T(8,128)(2,1)S(1)}, u32[]{:S(2)}, u32[]{:S(2)}) collective-permute-start(bf16[128,3072]{1,0:T(8,128)(2,1)S(1)} %get-tuple-element.51.mine_ref), channel_id=1, source_target_pairs={{0,4},{2,6},{4,8},{6,10},{8,12},{10,14},{12,0},{14,2},{1,5},{3,7},... | collective-permute-start | bytes 2359304 | tf_op jit(solution)/shard_map/ppermute | solution.py:211
  10.7 19.8 %collective-permute-start.9 = (bf16[4,8,2048]{2,1,0:T(8,128)(2,1)S(1)}, bf16[4,8,2048]{2,1,0:T(8,128)(2,1)S(1)}, u32[]{:S(2)}, u32[]{:S(2)}) collective-permute-start(bf16[4,8,2048]{2,1,0:T(8,128)(2,1)S(1)} %fusion.45), channel_id=1, source_target_pairs={{0,1},{1,0},{2,3},{3,2},{4,5},{5,4},{6,7},{7,6},{8,9},{9,8},{10,11... | collective-permute-start | bytes 393224 | tf_op jit(solution)/shard_map/ppermute | solution.py:33
  30.5 21.0 %collective-permute-start.5 = (bf16[128,3072]{1,0:T(8,128)(2,1)S(1)}, bf16[128,3072]{1,0:T(8,128)(2,1)S(1)}, u32[]{:S(2)}, u32[]{:S(2)}) collective-permute-start(bf16[128,3072]{1,0:T(8,128)(2,1)S(1)} %collective-permute-done.4.mine_ref), channel_id=1, source_target_pairs={{0,4},{2,6},{4,8},{6,10},{8,12},{10,14},{12,0},{14,2},{1,5},{3,7},... | collective-permute-start | bytes 2359304 | tf_op jit(solution)/shard_map/ppermute | solution.py:211
  30.7 31.0 %collective-permute-start.7 = (bf16[128,3072]{1,0:T(8,128)(2,1)S(1)}, bf16[128,3072]{1,0:T(8,128)(2,1)S(1)}, u32[]{:S(2)}, u32[]{:S(2)}) collective-permute-start(bf16[128,3072]{1,0:T(8,128)(2,1)S(1)} %collective-permute-done.4.mine_ref), channel_id=1, source_target_pairs={{0,16},{16,0},{1,17},{17,1},{2,18},{18,2},{3,19},{19,3},{4,20},{20... | collective-permute-start | bytes 2359304 | tf_op jit(solution)/shard_map/ppermute | solution.py:33
  44.3 12.6 %collective-permute-start.10 = (bf16[64,3,512]{2,1,0:T(4,128)(2,1)S(1)}, bf16[64,3,512]{2,1,0:T(4,128)(2,1)S(1)}, u32[]{:S(2)}, u32[]{:S(2)}) collective-permute-start(bf16[64,3,512]{2,1,0:T(4,128)(2,1)S(1)} %copy.30), channel_id=1, source_target_pairs={{0,16},{16,0},{1,17},{17,1},{2,18},{18,2},{3,19},{19,3},{4,20},{20... | collective-permute-start | bytes 589832 | tf_op jit(solution)/shard_map/ppermute | solution.py:33
  52.2 26.0 %collective-permute-start.13 = (bf16[128,3072]{1,0:T(8,128)(2,1)S(1)}, bf16[128,3072]{1,0:T(8,128)(2,1)S(1)}, u32[]{:S(2)}, u32[]{:S(2)}) collective-permute-start(bf16[128,3072]{1,0:T(8,128)(2,1)S(1)} %broadcast_add_fusion.1.mine_ref), channel_id=1, source_target_pairs={{0,16},{16,0},{1,17},{17,1},{2,18},{18,2},{3,19},{19,3},{4,20},{20... | collective-permute-start | bytes 2359304 | tf_op jit(solution)/shard_map/ppermute | solution.py:33
  52.3 35.6 %collective-permute-start.6 = (bf16[128,3072]{1,0:T(8,128)(2,1)S(1)}, bf16[128,3072]{1,0:T(8,128)(2,1)S(1)}, u32[]{:S(2)}, u32[]{:S(2)}) collective-permute-start(bf16[128,3072]{1,0:T(8,128)(2,1)S(1)} %broadcast_add_fusion.1.mine_ref), channel_id=1, source_target_pairs={{0,4},{2,6},{4,8},{6,10},{8,12},{10,14},{12,0},{14,2},{1,5},{3,7},... | collective-permute-start | bytes 2359304 | tf_op jit(solution)/shard_map/ppermute | solution.py:211
  56.8 21.4 %collective-permute-start.2 = (bf16[256,1536]{1,0:T(8,128)(2,1)S(1)}, bf16[256,1536]{1,0:T(8,128)(2,1)S(1)}, u32[]{:S(2)}, u32[]{:S(2)}) collective-permute-start(bf16[256,1536]{1,0:T(8,128)(2,1)S(1)} %get-tuple-element.22.own_ref), channel_id=1, source_target_pairs={{0,1},{1,0},{2,3},{3,2},{4,5},{5,4},{6,7},{7,6},{8,9},{9,8},{10,11... | collective-permute-start | bytes 2359304 | tf_op jit(solution)/shard_map/ppermute | solution.py:33
  70.5 7.7 %collective-permute-start.14 = (bf16[64,1664]{1,0:T(8,128)(2,1)S(1)}, bf16[64,1664]{1,0:T(8,128)(2,1)S(1)}, u32[]{:S(2)}, u32[]{:S(2)}) collective-permute-start(bf16[64,1664]{1,0:T(8,128)(2,1)S(1)} %maximum_add_fusion.2), channel_id=1, source_target_pairs={{0,4},{2,6},{4,8},{6,10},{8,12},{10,14},{12,0},{14,2},{1,5},{3,7},... | collective-permute-start | bytes 638984 | tf_op jit(solution)/shard_map/ppermute | solution.py:211
  71.5 22.6 %collective-permute-start.12 = (bf16[256,1536]{1,0:T(8,128)(2,1)S(1)}, bf16[256,1536]{1,0:T(8,128)(2,1)S(1)}, u32[]{:S(2)}, u32[]{:S(2)}) collective-permute-start(bf16[256,1536]{1,0:T(8,128)(2,1)S(1)} %get-tuple-element.25.own_ref), channel_id=1, source_target_pairs={{0,1},{1,0},{2,3},{3,2},{4,5},{5,4},{6,7},{7,6},{8,9},{9,8},{10,11... | collective-permute-start | bytes 2359304 | tf_op jit(solution)/shard_map/ppermute | solution.py:33
  78.2 24.7 %collective-permute-start.15 = (bf16[64,1664]{1,0:T(8,128)(2,1)S(1)}, bf16[64,1664]{1,0:T(8,128)(2,1)S(1)}, u32[]{:S(2)}, u32[]{:S(2)}) collective-permute-start(bf16[64,1664]{1,0:T(8,128)(2,1)S(1)} %collective-permute-done.14.refs_3_), channel_id=1, source_target_pairs={{0,4},{2,6},{4,8},{6,10},{8,12},{10,14},{12,0},{14,2},{1,5},{3,7},... | collective-permute-start | bytes 638984 | tf_op jit(solution)/shard_map/ppermute | solution.py:211
  85.7 33.5 %collective-permute-start.17 = (bf16[256,1536]{1,0:T(8,128)(2,1)S(1)}, bf16[256,1536]{1,0:T(8,128)(2,1)S(1)}, u32[]{:S(2)}, u32[]{:S(2)}) collective-permute-start(bf16[256,1536]{1,0:T(8,128)(2,1)S(1)} %get-tuple-element.29.own_ref), channel_id=1, source_target_pairs={{0,1},{1,0},{2,3},{3,2},{4,5},{5,4},{6,7},{7,6},{8,9},{9,8},{10,11... | collective-permute-start | bytes 2359304 | tf_op jit(solution)/shard_map/ppermute | solution.py:33
  88.6 23.1 %collective-permute-start.11 = (bf16[128,3072]{1,0:T(8,128)(2,1)S(1)}, bf16[128,3072]{1,0:T(8,128)(2,1)S(1)}, u32[]{:S(2)}, u32[]{:S(2)}) collective-permute-start(bf16[128,3072]{1,0:T(8,128)(2,1)S(1)} %broadcast_add_fusion.mine_ref), channel_id=1, source_target_pairs={{0,16},{16,0},{1,17},{17,1},{2,18},{18,2},{3,19},{19,3},{4,20},{20... | collective-permute-start | bytes 2359304 | tf_op jit(solution)/shard_map/ppermute | solution.py:33
  100.3 29.7 %collective-permute-start.23 = (bf16[128,3072]{1,0:T(8,128)(2,1)S(1)}, bf16[128,3072]{1,0:T(8,128)(2,1)S(1)}, u32[]{:S(2)}, u32[]{:S(2)}) collective-permute-start(bf16[128,3072]{1,0:T(8,128)(2,1)S(1)} %get-tuple-element.41), channel_id=1, source_target_pairs={{0,16},{16,0},{1,17},{17,1},{2,18},{18,2},{3,19},{19,3},{4,20},{20... | collective-permute-start | bytes 2359304 | tf_op jit(solution)/shard_map/ppermute | solution.py:33
  102.9 7.9 %collective-permute-start.18 = (bf16[64,1664]{1,0:T(8,128)(2,1)S(1)}, bf16[64,1664]{1,0:T(8,128)(2,1)S(1)}, u32[]{:S(2)}, u32[]{:S(2)}) collective-permute-start(bf16[64,1664]{1,0:T(8,128)(2,1)S(1)} %collective-permute-done.15.refs_3_), channel_id=1, source_target_pairs={{0,4},{2,6},{4,8},{6,10},{8,12},{10,14},{12,0},{14,2},{1,5},{3,7},... | collective-permute-start | bytes 638984 | tf_op jit(solution)/shard_map/ppermute | solution.py:211
  111.8 46.5 %collective-permute-start.19 = (bf16[256,1664]{1,0:T(8,128)(2,1)}, bf16[256,1664]{1,0:T(8,128)(2,1)S(1)}, u32[]{:S(2)}, u32[]{:S(2)}) collective-permute-start(bf16[256,1664]{1,0:T(8,128)(2,1)} %pad_maximum_fusion), channel_id=1, source_target_pairs={{0,2},{2,0},{4,6},{6,4},{8,10},{10,8},{12,14},{14,12},{1,3},{3,1},... | collective-permute-start | bytes 2555912 | tf_op jit(solution)/shard_map/ppermute | solution.py:348
  128.0 37.1 %collective-permute-start.22 = (bf16[128,3072]{1,0:T(8,128)(2,1)}, bf16[128,3072]{1,0:T(8,128)(2,1)}, u32[]{:S(2)}, u32[]{:S(2)}) collective-permute-start(bf16[128,3072]{1,0:T(8,128)(2,1)} %get-tuple-element.39), channel_id=1, source_target_pairs={{0,16},{16,0},{1,17},{17,1},{2,18},{18,2},{3,19},{19,3},{4,20},{20... | collective-permute-start | bytes 2359304 | tf_op jit(solution)/shard_map/ppermute | solution.py:33
  130.0 19.7 %collective-permute-start.16 = (bf16[256,1536]{1,0:T(8,128)(2,1)S(1)}, bf16[256,1536]{1,0:T(8,128)(2,1)S(1)}, u32[]{:S(2)}, u32[]{:S(2)}) collective-permute-start(bf16[256,1536]{1,0:T(8,128)(2,1)S(1)} %get-tuple-element.28.own_ref), channel_id=1, source_target_pairs={{0,1},{1,0},{2,3},{3,2},{4,5},{5,4},{6,7},{7,6},{8,9},{9,8},{10,11... | collective-permute-start | bytes 2359304 | tf_op jit(solution)/shard_map/ppermute | solution.py:33
  131.8 33.3 %collective-permute-start.24 = (bf16[128,3072]{1,0:T(8,128)(2,1)}, bf16[128,3072]{1,0:T(8,128)(2,1)}, u32[]{:S(2)}, u32[]{:S(2)}) collective-permute-start(bf16[128,3072]{1,0:T(8,128)(2,1)} %add_convert_fusion.2), channel_id=1, source_target_pairs={{0,4},{2,6},{4,8},{6,10},{8,12},{10,14},{12,0},{14,2},{1,5},{3,7},... | collective-permute-start | bytes 2359304 | tf_op jit(solution)/shard_map/ppermute | solution.py:211
  158.0 20.8 %collective-permute-start.21 = (bf16[128,3072]{1,0:T(8,128)(2,1)}, bf16[128,3072]{1,0:T(8,128)(2,1)}, u32[]{:S(2)}, u32[]{:S(2)}) collective-permute-start(bf16[128,3072]{1,0:T(8,128)(2,1)} %get-tuple-element.37), channel_id=1, source_target_pairs={{0,16},{16,0},{1,17},{17,1},{2,18},{18,2},{3,19},{19,3},{4,20},{20... | collective-permute-start | bytes 2359304 | tf_op jit(solution)/shard_map/ppermute | solution.py:33
  168.3 21.0 %collective-permute-start.25 = (bf16[128,3072]{1,0:T(8,128)(2,1)}, bf16[128,3072]{1,0:T(8,128)(2,1)S(1)}, u32[]{:S(2)}, u32[]{:S(2)}) collective-permute-start(bf16[128,3072]{1,0:T(8,128)(2,1)} %add_convert_fusion.1), channel_id=1, source_target_pairs={{0,4},{2,6},{4,8},{6,10},{8,12},{10,14},{12,0},{14,2},{1,5},{3,7},... | collective-permute-start | bytes 2359304 | tf_op jit(solution)/shard_map/ppermute | solution.py:211
  172.0 23.0 %collective-permute-start.20 = (bf16[128,3072]{1,0:T(8,128)(2,1)}, bf16[128,3072]{1,0:T(8,128)(2,1)}, u32[]{:S(2)}, u32[]{:S(2)}) collective-permute-start(bf16[128,3072]{1,0:T(8,128)(2,1)} %copy-done.9), channel_id=1, source_target_pairs={{0,16},{16,0},{1,17},{17,1},{2,18},{18,2},{3,19},{19,3},{4,20},{20... | collective-permute-start | bytes 2359304 | tf_op jit(solution)/shard_map/ppermute | solution.py:33
  194.0 20.2 %collective-permute-start.26 = (bf16[128,3072]{1,0:T(8,128)(2,1)}, bf16[128,3072]{1,0:T(8,128)(2,1)}, u32[]{:S(2)}, u32[]{:S(2)}) collective-permute-start(bf16[128,3072]{1,0:T(8,128)(2,1)} %add_convert_fusion), channel_id=1, source_target_pairs={{0,4},{2,6},{4,8},{6,10},{8,12},{10,14},{12,0},{14,2},{1,5},{3,7},... | collective-permute-start | bytes 2359304 | tf_op jit(solution)/shard_map/ppermute | solution.py:211
  216.1 17.2 %collective-permute-start.27 = (bf16[128,3072]{1,0:T(8,128)(2,1)S(1)}, bf16[128,3072]{1,0:T(8,128)(2,1)S(1)}, u32[]{:S(2)}, u32[]{:S(2)}) collective-permute-start(bf16[128,3072]{1,0:T(8,128)(2,1)S(1)} %fusion.20), channel_id=1, source_target_pairs={{0,16},{16,0},{1,17},{17,1},{2,18},{18,2},{3,19},{19,3},{4,20},{20... | collective-permute-start | bytes 2359304 | tf_op jit(solution)/shard_map/ppermute | solution.py:33
  224.8 16.2 %collective-permute-start.28 = (bf16[128,2048]{1,0:T(8,128)(2,1)}, bf16[128,2048]{1,0:T(8,128)(2,1)}, u32[]{:S(2)}, u32[]{:S(2)}) collective-permute-start(bf16[128,2048]{1,0:T(8,128)(2,1)} %get-tuple-element.68), channel_id=1, source_target_pairs={{0,1},{1,0},{2,3},{3,2},{4,5},{5,4},{6,7},{7,6},{8,9},{9,8},{10,11... | collective-permute-start | bytes 1572872 | tf_op jit(solution)/shard_map/ppermute | solution.py:33
  236.3 11.0 %collective-permute-start.29 = (bf16[128,2048]{1,0:T(8,128)(2,1)}, bf16[128,2048]{1,0:T(8,128)(2,1)}, u32[]{:S(2)}, u32[]{:S(2)}) collective-permute-start(bf16[128,2048]{1,0:T(8,128)(2,1)} %get-tuple-element.70), channel_id=1, source_target_pairs={{0,1},{1,0},{2,3},{3,2},{4,5},{5,4},{6,7},{7,6},{8,9},{9,8},{10,11... | collective-permute-start | bytes 1572872 | tf_op jit(solution)/shard_map/ppermute | solution.py:33
  249.0 10.3 %collective-permute-start.33 = (f32[128]{0:T(128)S(1)}, f32[128]{0:T(128)S(1)}, u32[]{:S(2)}, u32[]{:S(2)}) collective-permute-start(f32[128]{0:T(128)S(1)} %get-tuple-element.48), channel_id=1, source_target_pairs={{0,16},{16,0},{1,17},{17,1},{2,18},{18,2},{3,19},{19,3},{4,20},{20... | collective-permute-start | bytes 1544 | tf_op jit(solution)/shard_map/ppermute | solution.py:33
  250.2 9.1 %collective-permute-start.31 = (f32[128]{0:T(128)S(1)}, f32[128]{0:T(128)S(1)}, u32[]{:S(2)}, u32[]{:S(2)}) collective-permute-start(f32[128]{0:T(128)S(1)} %get-tuple-element.64), channel_id=1, source_target_pairs={{0,16},{16,0},{1,17},{17,1},{2,18},{18,2},{3,19},{19,3},{4,20},{20... | collective-permute-start | bytes 1544 | tf_op jit(solution)/shard_map/ppermute | solution.py:33
  258.2 8.5 %collective-permute-start.32 = (bf16[128,2,512]{2,0,1:T(8,128)(2,1)S(1)}, bf16[128,2,512]{2,0,1:T(8,128)(2,1)S(1)}, u32[]{:S(2)}, u32[]{:S(2)}) collective-permute-start(bf16[128,2,512]{2,0,1:T(8,128)(2,1)S(1)} %fusion.24), channel_id=1, source_target_pairs={{0,16},{16,0},{1,17},{17,1},{2,18},{18,2},{3,19},{19,3},{4,20},{20... | collective-permute-start | bytes 786440 | tf_op jit(solution)/shard_map/ppermute | solution.py:33
  275.7 7.2 %collective-permute-start.35 = (bf16[128,512]{1,0:T(8,128)(2,1)S(1)}, bf16[128,512]{1,0:T(8,128)(2,1)S(1)}, u32[]{:S(2)}, u32[]{:S(2)}) collective-permute-start(bf16[128,512]{1,0:T(8,128)(2,1)S(1)} %get-tuple-element.57), channel_id=1, source_target_pairs={{0,8},{2,10},{4,12},{6,14},{8,0},{10,2},{12,4},{14,6},{1,9},{3,11}... | collective-permute-start | bytes 393224 | tf_op jit(solution)/shard_map/ppermute | solution.py:211
  (36 other events, 318.7 us)
